TPU v7x, 128 devices: a whole 4x4x4 slice. The times are simulated.
128 devices in a mesh: pipe: 2 (over core), tensor: 4 (over x), dp: 16 (over z, y).
Axes of the slice: x: 4, y: 4, z: 4, core: 2. Of those that a mesh axis runs over, the one named last changes fastest.
Arguments:
- x_saved: bfloat16 [2, 16, 2, 256, 4096], P('pipe', 'dp', None, 'tensor'), may hold values from -6 to 6
- grad_top: bfloat16 [2, 16, 256, 4096], P('pipe', 'dp', 'tensor'), may hold values from -6 to 6
- query: bfloat16 [2, 16, 2, 256, 4096], P('pipe', 'dp', None, None, 'tensor'), may hold values from -16 to 16
- key: bfloat16 [2, 16, 2, 256, 1024], P('pipe', 'dp', None, None, 'tensor'), may hold values from -16 to 16
- value: bfloat16 [2, 16, 2, 256, 1024], P('pipe', 'dp', None, None, 'tensor'), may hold values from -6 to 6
- segment: int32 [2, 16, 2, 256], P('pipe', 'dp'), may hold values from 0 to 3, never falling along the last dimension, each value on 1 to 128 neighbouring positions
- w_query: bfloat16 [2, 4096, 4096], P('pipe', 'dp', 'tensor'), may hold values from -0.09375 to 0.09375
- key_weight: bfloat16 [2, 4096, 1024], P('pipe', 'dp', 'tensor'), may hold values from -0.09375 to 0.09375
- value_weight: bfloat16 [2, 4096, 1024], P('pipe', 'dp', 'tensor'), may hold values from -0.09375 to 0.09375
- w_out: bfloat16 [2, 4096, 4096], P('pipe', 'dp', 'tensor'), may hold values from -0.09375 to 0.09375
- gain: float32 [2, 4096], P('pipe'), may hold values from 0.1 to 1.9
Outputs:
- grad_bottom: bfloat16 [2, 16, 256, 4096], P('pipe', 'dp', 'tensor')
- grad_query: bfloat16 [2, 4096, 4096], P('pipe', 'dp', 'tensor')
- grad_key: bfloat16 [2, 4096, 1024], P('pipe', 'dp', 'tensor')
- grad_value: bfloat16 [2, 4096, 1024], P('pipe', 'dp', 'tensor')
- grad_out: bfloat16 [2, 4096, 4096], P('pipe', 'dp', 'tensor')
- grad_gain: float32 [2, 4096], P('pipe')
Inputs may be any that keep to these rules, and one draw needn't show every extreme that they name: `segment`: document ids never fall along a micro-batch.
All inputs are finite; a program needn't handle non-finite values.
Results may differ from a plain program's by a relative error of at most 0.029.
Values may be sent and summed in bfloat16 or wider, within the bound.
A program may use at most 384 MiB of HBM per device.

v0:
```python
import math

import jax
import jax.numpy as jnp
from jax import lax
from jax.sharding import PartitionSpec as P

HEAD_SIZE = 128


NORM_EPSILON = 1e-05


def passed_along(value, axis, steps):
    count = lax.axis_size(axis)
    pairs = [(source, (source + steps) % count) for source in range(count)]
    return lax.ppermute(value, axis, pairs)


def across(left, right):
    return lax.dot_general(
        left, right, (((0,), (0,)), ((), ())), preferred_element_type=jnp.float32
    )


def against(left, right):
    return lax.dot_general(
        left, right, (((1,), (1,)), ((), ())), preferred_element_type=jnp.float32
    )


def split_heads(query_row_block, key_row_block, value_row_block):
    token_length = query_row_block.shape[0]
    kv_count = key_row_block.shape[1] // HEAD_SIZE
    query_group_width = query_row_block.shape[1] // key_row_block.shape[1]
    return (
        query_row_block.reshape(token_length, kv_count, query_group_width, HEAD_SIZE),
        key_row_block.reshape(token_length, kv_count, HEAD_SIZE),
        value_row_block.reshape(token_length, kv_count, HEAD_SIZE),
    )


def attention_forward(query_row_block, key_row_block, value_row_block, segment_ids):
    query_head_split, key_head_split, value_head_split = split_heads(
        query_row_block, key_row_block, value_row_block
    )
    token_length = query_row_block.shape[0]
    score_scale = 1.0 / math.sqrt(HEAD_SIZE)
    scores = (
        jnp.einsum(
            "ikgd,jkd->kgij", query_head_split, key_head_split, preferred_element_type=jnp.float32
        )
        * score_scale
    )
    row_ids = lax.broadcasted_iota(jnp.int32, (token_length, token_length), 0)
    col_ids = lax.broadcasted_iota(jnp.int32, (token_length, token_length), 1)
    allowed = (col_ids <= row_ids) & (segment_ids[:, None] == segment_ids[None, :])
    scores = jnp.where(allowed, scores, -jnp.inf)
    attention = jax.nn.softmax(scores, axis=-1)
    attention_second = attention.astype(jnp.bfloat16)
    attended = jnp.einsum(
        "kgij,jkd->ikgd", attention_second, value_head_split, preferred_element_type=jnp.float32
    )
    return (attention, attention_second, attended.astype(jnp.bfloat16).reshape(token_length, -1))


def attention_backward(
    query_row_block, key_row_block, value_row_block, attention, attention_second, attention_gradient
):
    query_head_split, key_head_split, value_head_split = split_heads(
        query_row_block, key_row_block, value_row_block
    )
    token_length = query_row_block.shape[0]
    score_scale = 1.0 / math.sqrt(HEAD_SIZE)
    head_gradient = attention_gradient.reshape(query_head_split.shape)
    grad_probs = jnp.einsum(
        "ikgd,jkd->kgij", head_gradient, value_head_split, preferred_element_type=jnp.float32
    )
    row_dot = jnp.sum(attention * grad_probs, axis=-1, keepdims=True)
    score_gradient = (attention * (grad_probs - row_dot) * score_scale).astype(jnp.bfloat16)
    grad_q = jnp.einsum(
        "kgij,jkd->ikgd", score_gradient, key_head_split, preferred_element_type=jnp.float32
    )
    key_gradient = jnp.einsum(
        "eshv,hest->vet", score_gradient, query_head_split, preferred_element_type=jnp.float32
    )
    value_gradient = jnp.einsum(
        "eshv,hest->vet", attention_second, head_gradient, preferred_element_type=jnp.float32
    )
    return (
        grad_q.astype(jnp.bfloat16).reshape(token_length, -1),
        key_gradient.astype(jnp.bfloat16).reshape(token_length, -1),
        value_gradient.astype(jnp.bfloat16).reshape(token_length, -1),
    )


def local(
    x_saved, grad_top, query, key, value, segment, w_query, key_weight, value_weight, w_out, gain
):
    saved_rows = x_saved[0, 0]
    top_grad = grad_top[0, 0]
    query_row_block = query[0, 0]
    key_row_block = key[0, 0]
    value_row_block = value[0, 0]
    segment_ids = segment[0, 0]
    gain_row = gain[0]
    full_query, full_key, full_value, full_out = (
        lax.all_gather(w_query[0], "dp", axis=0, tiled=True),
        lax.all_gather(key_weight[0], "dp", axis=0, tiled=True),
        lax.all_gather(value_weight[0], "dp", axis=0, tiled=True),
        lax.all_gather(w_out[0], "dp", axis=0, tiled=True),
    )

    def backward(batch_index, upstream_part):
        attention, attention_second, attended = attention_forward(
            query_row_block[batch_index],
            key_row_block[batch_index],
            value_row_block[batch_index],
            segment_ids[batch_index],
        )
        x_float = saved_rows[batch_index].astype(jnp.float32)
        inv_rms = lax.rsqrt(jnp.mean(x_float * x_float, axis=-1, keepdims=True) + NORM_EPSILON)
        unit_rows = x_float * inv_rms
        normed = (unit_rows * gain_row).astype(jnp.bfloat16)
        normed_full, upstream = (
            lax.all_gather(normed, "tensor", axis=0, tiled=True),
            lax.all_gather(upstream_part, "tensor", axis=0, tiled=True),
        )
        attention_gradient = jnp.dot(upstream, full_out, preferred_element_type=jnp.float32).astype(
            jnp.bfloat16
        )
        grad_q, key_gradient, value_gradient = attention_backward(
            query_row_block[batch_index],
            key_row_block[batch_index],
            value_row_block[batch_index],
            attention,
            attention_second,
            attention_gradient,
        )
        total = against(grad_q, full_query)
        total = total + against(key_gradient, full_key)
        grad_normed = lax.psum_scatter(
            (total + against(value_gradient, full_value)).astype(jnp.bfloat16),
            "tensor",
            scatter_dimension=0,
            tiled=True,
        ).astype(jnp.float32)
        scaled = gain_row * grad_normed
        grad_input = upstream_part.astype(jnp.float32) + inv_rms * (
            scaled - unit_rows * jnp.mean(unit_rows * scaled, axis=-1, keepdims=True)
        )
        gain_term = jnp.sum(grad_normed * unit_rows, axis=0)
        return (
            grad_input.astype(jnp.bfloat16),
            gain_term,
            (normed_full, upstream, grad_q, key_gradient, value_gradient, attended),
        )

    first_grad, gain_first, rows_first = backward(0, top_grad)
    arrived = passed_along(first_grad, "pipe", -1)
    second_grad, gain_second, rows_second = backward(1, arrived)
    stacked = tuple(
        (
            jnp.concatenate([first_part, second_part], axis=0)
            for first_part, second_part in zip(rows_first, rows_second)
        )
    )
    normed_all, upstream_all, query_all, key_all, value_all, attended_all = stacked
    summed = (
        lax.psum_scatter(
            across(normed_all, query_all).astype(jnp.bfloat16),
            "dp",
            scatter_dimension=0,
            tiled=True,
        ).astype(jnp.float32),
        lax.psum_scatter(
            across(normed_all, key_all).astype(jnp.bfloat16), "dp", scatter_dimension=0, tiled=True
        ).astype(jnp.float32),
        lax.psum_scatter(
            across(normed_all, value_all).astype(jnp.bfloat16),
            "dp",
            scatter_dimension=0,
            tiled=True,
        ).astype(jnp.float32),
        lax.psum_scatter(
            across(upstream_all, attended_all).astype(jnp.bfloat16),
            "dp",
            scatter_dimension=0,
            tiled=True,
        ).astype(jnp.float32),
    )
    gain_total = lax.psum(gain_first + gain_second, ("tensor", "dp"))
    grad_weights = tuple((piece.astype(jnp.bfloat16)[None] for piece in summed))
    return (
        second_grad[None, None],
        grad_weights[0],
        grad_weights[1],
        grad_weights[2],
        grad_weights[3],
        gain_total[None],
    )


def solution(mesh):
    in_specs = (
        P("pipe", "dp", None, "tensor", None),
        P("pipe", "dp", "tensor", None),
        P("pipe", "dp", None, None, "tensor"),
        P("pipe", "dp", None, None, "tensor"),
        P("pipe", "dp", None, None, "tensor"),
        P("pipe", "dp", None, None),
        P("pipe", "dp", "tensor"),
        P("pipe", "dp", "tensor"),
        P("pipe", "dp", "tensor"),
        P("pipe", "dp", "tensor"),
        P("pipe", None),
    )
    out_specs = (
        P("pipe", "dp", "tensor", None),
        P("pipe", "dp", "tensor"),
        P("pipe", "dp", "tensor"),
        P("pipe", "dp", "tensor"),
        P("pipe", "dp", "tensor"),
        P("pipe", None),
    )
    return jax.shard_map(local, mesh=mesh, in_specs=in_specs, out_specs=out_specs, check_vma=False)
```

profile of v0, /device:TPU:0, one launch (start us, length us, event | category | flops | bytes accessed | tf_op | source)
XLA Modules:
  0.0 871.1 jit_solution(14727015742110617498)
XLA Ops:
  7.2 0.7 all-gather.20.cloned.1.call-update
  8.0 0.7 all-gather.22.cloned.1.call-update
  8.7 0.7 all-gather.24.cloned.1.call-update
  9.5 0.5 all-gather.26.cloned.1.call-update
  10.0 0.5 all-gather.28.cloned.1.call-update
  11.3 0.6 fusion.114
  12.0 2.1 fusion.115
  14.1 28.9 %all-gather.20.cloned.1.call-done = bf16[1,1,256,4096]{3,2,1,0:T(8,128)(2,1)} async-done(((bf16[1,1,64,4096]{3,2,1,0:T(8,128)(2,1)}), bf16[1,1,256,4096]{3,2,1,0:T(8,128)(2,1)}) %all-gather.20.cloned.1.call-update) | async-done | bytes 2097168 | tf_op jit(solution)/shard_map/all_gather | solution.py:127
  43.0 73.1 %all-gather.22.cloned.1.call-done = bf16[1,4096,1024]{2,1,0:T(8,128)(2,1)} async-done(((bf16[1,256,1024]{2,1,0:T(8,128)(2,1)}), bf16[1,4096,1024]{2,1,0:T(8,128)(2,1)}) %all-gather.22.cloned.1.call-update) | async-done | bytes 8388624 | tf_op jit(solution)/shard_map/all_gather | solution.py:111
  116.1 6.3 fusion.37
  122.4 0.2 copy.95
  122.6 0.5 fusion.117
  123.1 3.9 convolution_convert_fusion.7
  127.0 4.1 fusion.45
  131.1 2.1 fusion.46
  133.2 55.6 %all-gather.24.cloned.1.call-done = bf16[1,4096,1024]{2,1,0:T(8,128)(2,1)} async-done(((bf16[1,256,1024]{2,1,0:T(8,128)(2,1)}), bf16[1,4096,1024]{2,1,0:T(8,128)(2,1)}) %all-gather.24.cloned.1.call-update) | async-done | bytes 8388624 | tf_op jit(solution)/shard_map/all_gather | solution.py:108
  188.8 7.8 fusion.6
  196.6 39.1 %all-gather.26.cloned.1.call-done = bf16[1,4096,256]{2,1,0:T(8,128)(2,1)} async-done(((bf16[1,256,256]{2,1,0:T(8,128)(2,1)}), bf16[1,4096,256]{2,1,0:T(8,128)(2,1)}) %all-gather.26.cloned.1.call-update) | async-done | bytes 2097168 | tf_op jit(solution)/shard_map/all_gather | solution.py:109
  235.7 5.5 convolution_add_fusion.3
  241.2 41.0 %all-gather.28.cloned.1.call-done = bf16[1,4096,256]{2,1,0:T(8,128)(2,1)} async-done(((bf16[1,256,256]{2,1,0:T(8,128)(2,1)}), bf16[1,4096,256]{2,1,0:T(8,128)(2,1)}) %all-gather.28.cloned.1.call-update) | async-done | bytes 2097168 | tf_op jit(solution)/shard_map/all_gather | solution.py:110
  282.3 5.0 fusion.12
  287.3 1.1 copy-done
  288.4 0.2 fusion.58
  288.7 27.6 %reduce-scatter.7.cloned.1.call-done = bf16[64,4096]{1,0:T(8,128)(2,1)} async-done(((bf16[256,4096]{1,0:T(8,128)(2,1)}), bf16[64,4096]{1,0:T(8,128)(2,1)}) %reduce-scatter.7.cloned.1.call-update) | async-done | bytes 524304 | tf_op jit(solution)/shard_map/reduce_scatter | solution.py:142
  316.3 2.1 fusion.57
  318.4 2.3 fusion.56
  320.7 1.9 collective-permute-done
  322.6 0.8 copy-done.4
  323.4 0.2 reduce-scatter.9.cloned.1.call-start
  323.6 0.8 copy.94
  324.8 2.8 fusion.116
  327.6 26.5 %all-gather.14.cloned.1.call-done = bf16[256,4096]{1,0:T(8,128)(2,1)} async-done(((bf16[64,4096]{1,0:T(8,128)(2,1)}), bf16[256,4096]{1,0:T(8,128)(2,1)}) %all-gather.14.cloned.1.call-update) | async-done | bytes 2097168 | tf_op jit(solution)/shard_map/all_gather | solution.py:127
  354.1 6.3 fusion.40
  360.4 1.0 copy.96
  361.5 1.5 fusion.118
  363.0 3.8 fusion.47
  366.8 3.8 convolution_convert_fusion.6
  370.6 2.2 fusion.48
  372.9 5.9 fusion.4
  378.8 0.8 convolution_add_fusion.1
  379.6 0.8 copy-done.2
  380.4 2.1 fusion.13
  382.6 0.7 all-gather.16.cloned.1.call-update
  383.3 29.0 %reduce-scatter.9.cloned.1.call-done = bf16[64,4096]{1,0:T(8,128)(2,1)} async-done(((bf16[256,4096]{1,0:T(8,128)(2,1)}), bf16[64,4096]{1,0:T(8,128)(2,1)}) %reduce-scatter.9.cloned.1.call-update) | async-done | bytes 524304 | tf_op jit(solution)/shard_map/reduce_scatter | solution.py:142
  412.3 2.3 fusion.61
  414.8 30.4 %all-gather.16.cloned.1.call-done = bf16[256,4096]{1,0:T(8,128)(2,1)} async-done(((bf16[64,4096]{1,0:T(8,128)(2,1)}), bf16[256,4096]{1,0:T(8,128)(2,1)}) %all-gather.16.cloned.1.call-update) | async-done | bytes 2097168 | tf_op jit(solution)/shard_map/all_gather | solution.py:126
  445.2 3.1 constant_dynamic-update-slice_fusion.1
  448.3 29.2 %all-gather.18.cloned.1.call-done = bf16[256,4096]{1,0:T(8,128)(2,1)} async-done(((bf16[64,4096]{1,0:T(8,128)(2,1)}), bf16[256,4096]{1,0:T(8,128)(2,1)}) %all-gather.18.cloned.1.call-update) | async-done | bytes 2097168 | tf_op jit(solution)/shard_map/all_gather | solution.py:126
  477.6 3.2 constant_dynamic-update-slice_fusion
  480.8 4.8 convolution_convert_fusion.2
  485.6 0.3 reduce-scatter.13.cloned.1.call-start
  485.9 0.6 copy-done.18
  486.5 4.8 convolution_convert_fusion.3
  491.4 0.6 copy-done.31
  492.0 2.1 convolution_convert_fusion.5
  494.2 0.3 convolution_convert_fusion.4
  494.6 1.3 copy-done.24
  495.9 0.6 copy-done.25
  496.6 6.9 convolution_convert_fusion
  503.5 1.0 copy-done.27
  504.5 9.1 %convolution_convert_fusion.1 = bf16[4096,1024]{1,0:T(8,128)(2,1)} fusion(bf16[512,4096]{1,0:T(8,128)(2,1)} %constant_dynamic-update-slice_fusion, bf16[256,1024]{0,1:T(8,128)(2,1)S(1)} %bitcast.251, bf16[256,1024]{0,1:T(8,128)(2,1)S(1)} %bitcast.249), kind=kOutput, calls=%fused_computation.13 | convolution fusion | flops 4301258752 | bytes 13631488 | tf_op jit(solution)/shard_map/dot_general | solution.py:21
  513.6 0.7 copy-done.20
  514.3 349.0 %psum.7 = f32[1,4096]{1,0:T(1,128)} all-reduce(f32[1,4096]{1,0:T(1,128)S(1)} %bitcast.240), channel_id=1, replica_groups=mesh['pipe'=2,'tensor'=4,'dp'=16] {'tensor','dp'}, use_global_device_ids=true, to_apply=%region_18.19 | all-reduce | flops 4096 | bytes 32768 | tf_op jit(solution)/shard_map/psum | solution.py:192
  863.4 1.2 fusion.77
  (97 shorter events, 2.0 us)
Async XLA Ops:
  7.2 3.5 copy-start.7
  7.2 3.5 copy-start.12
  7.2 3.6 copy-start.13
  7.2 35.8 %all-gather.20.cloned.1.call-start = ((), (), s32[]{:S(2)}) async-start(), calls=%async_computation.15 | async-start | bytes 2621440 | tf_op jit(solution)/shard_map/all_gather | solution.py:127
  7.9 108.1 %all-gather.22.cloned.1.call-start = ((), (), s32[]{:S(2)}) async-start(), calls=%async_computation.16 | async-start | bytes 8912896 | tf_op jit(solution)/shard_map/all_gather | solution.py:111
  8.7 180.1 %all-gather.24.cloned.1.call-start = ((), (), s32[]{:S(2)}) async-start(), calls=%async_computation.17 | async-start | bytes 8912896 | tf_op jit(solution)/shard_map/all_gather | solution.py:108
  9.4 226.3 %all-gather.26.cloned.1.call-start = ((), (), s32[]{:S(2)}) async-start(), calls=%async_computation.18 | async-start | bytes 2228224 | tf_op jit(solution)/shard_map/all_gather | solution.py:109
  10.0 272.3 %all-gather.28.cloned.1.call-start = ((), (), s32[]{:S(2)}) async-start(), calls=%async_computation.19 | async-start | bytes 2228224 | tf_op jit(solution)/shard_map/all_gather | solution.py:110
  10.6 0.7 copy-start.22
  10.6 305.7 %reduce-scatter.7.cloned.1.call-start = ((), (), s32[]{:S(2)}) async-start(), calls=%async_computation.6 | async-start | bytes 2621440 | tf_op jit(solution)/shard_map/reduce_scatter | solution.py:142
  11.0 3.1 copy-start.8
  11.1 2.9 copy-start.16
  14.1 117.0 %copy-start.30 = (f32[2,4,256]{2,1,0:T(4,128)}, f32[2,4,256]{2,1,0:T(4,128)S(1)}, u32[]{:S(2)}) copy-start(f32[2,4,256]{2,1,0:T(4,128)S(1)} %get-tuple-element.22) | copy-start | bytes 24580
  131.0 57.7 %copy-start.26 = (bf16[2,4,256,128]{2,3,1,0:T(8,128)(2,1)S(1)}, bf16[2,4,256,128]{2,3,1,0:T(8,128)(2,1)}, u32[]{:S(2)}) copy-start(bf16[2,4,256,128]{2,3,1,0:T(8,128)(2,1)} %convolution_convert_fusion.7) | copy-start | bytes 1572868
  133.2 149.1 %copy-start.14 = (bf16[2,128,256]{2,1,0:T(8,128)(2,1)}, bf16[2,128,256]{2,1,0:T(8,128)(2,1)S(1)}, u32[]{:S(2)}) copy-start(bf16[2,128,256]{2,1,0:T(8,128)(2,1)S(1)} %fusion.46) | copy-start | bytes 393220
  188.8 46.9 %copy-start.17 = (bf16[2,256,128]{1,2,0:T(8,128)(2,1)S(1)}, bf16[2,256,128]{1,2,0:T(8,128)(2,1)}, u32[]{:S(2)}) copy-start(bf16[2,256,128]{1,2,0:T(8,128)(2,1)} %fusion.45) | copy-start | bytes 393220
  287.2 1.2 copy-start
  287.2 29.1 %copy-start.11 = (f32[1,4096]{1,0:T(1,128)S(1)}, f32[1,4096]{1,0:T(1,128)}, u32[]{:S(2)}) copy-start(f32[1,4096]{1,0:T(1,128)} %param.21) | copy-start | bytes 49156
  287.2 31.2 %copy-start.3 = (bf16[1,1,64,4096]{3,2,1,0:T(8,128)(2,1)S(1)}, bf16[1,1,64,4096]{3,2,1,0:T(8,128)(2,1)}, u32[]{:S(2)}) copy-start(bf16[1,1,64,4096]{3,2,1,0:T(8,128)(2,1)} %param.12) | copy-start | bytes 1572868
  287.2 66.8 %all-gather.14.cloned.1.call-start = ((), (), s32[]{:S(2)}) async-start(), calls=%async_computation.7 | async-start | bytes 2621440 | tf_op jit(solution)/shard_map/all_gather | solution.py:127
  318.4 6.3 copy-start.21
  320.7 1.9 collective-permute-start
  322.6 0.8 copy-start.4
  323.4 88.9 %reduce-scatter.9.cloned.1.call-start = ((), (), s32[]{:S(2)}) async-start(), calls=%async_computation.8 | async-start | bytes 2621440 | tf_op jit(solution)/shard_map/reduce_scatter | solution.py:142
  324.6 3.0 copy-start.9
  327.6 33.9 %copy-start.10 = (bf16[1,1,1,256,256]{3,4,2,1,0:T(8,128)(2,1)S(1)}, bf16[1,1,1,256,256]{3,4,2,1,0:T(8,128)(2,1)}, u32[]{:S(2)}) copy-start(bf16[1,1,1,256,256]{3,4,2,1,0:T(8,128)(2,1)} %copy.94) | copy-start | bytes 393220
  370.6 2.2 copy-start.28
  372.8 6.0 copy-start.1
  372.8 6.0 copy-start.19
  378.8 1.6 copy-start.2
  382.5 0.8 copy-start.23
  382.5 62.7 %all-gather.16.cloned.1.call-start = ((), (), s32[]{:S(2)}) async-start(), calls=%async_computation.9 | async-start | bytes 2621440 | tf_op jit(solution)/shard_map/all_gather | solution.py:126
  383.3 94.3 %all-gather.18.cloned.1.call-start = ((), (), s32[]{:S(2)}) async-start(), calls=%async_computation.10 | async-start | bytes 2621440 | tf_op jit(solution)/shard_map/all_gather | solution.py:126
  414.7 449.8 %reduce-scatter.15.cloned.1.call-start = ((), (), s32[]{:S(2)}) async-start(), calls=%async_computation.13 | async-start | bytes 2228224 | tf_op jit(solution)/shard_map/reduce_scatter | solution.py:179
  448.3 32.5 %copy-start.15 = (bf16[2,128,256]{2,1,0:T(8,128)(2,1)S(1)}, bf16[2,128,256]{2,1,0:T(8,128)(2,1)}, u32[]{:S(2)}) copy-start(bf16[2,128,256]{2,1,0:T(8,128)(2,1)} %copy-done.14) | copy-start | bytes 393220
  485.6 0.9 copy-start.18
  485.6 378.9 %reduce-scatter.13.cloned.1.call-start = ((), (), s32[]{:S(2)}) async-start(), calls=%async_computation.12 | async-start | bytes 2228224 | tf_op jit(solution)/shard_map/reduce_scatter | solution.py:176
  491.3 0.7 copy-start.31
  491.3 2.7 copy-start.32
  491.3 373.2 %reduce-scatter.17.cloned.1.call-start = ((), (), s32[]{:S(2)}) async-start(), calls=%async_computation.14 | async-start | bytes 8912896 | tf_op jit(solution)/shard_map/reduce_scatter | solution.py:185
  492.0 2.2 copy-start.29
  494.2 1.7 copy-start.24
  494.2 2.3 copy-start.25
  503.4 1.0 copy-start.27
  503.4 361.1 %reduce-scatter.11.cloned.1.call-start = ((), (), s32[]{:S(2)}) async-start(), calls=%async_computation.11 | async-start | bytes 8912896 | tf_op jit(solution)/shard_map/reduce_scatter | solution.py:170
  513.6 0.7 copy-start.20
  513.6 349.8 %copy-start.5 = (bf16[64,4096]{1,0:T(8,128)(2,1)S(1)}, bf16[64,4096]{1,0:T(8,128)(2,1)}, u32[]{:S(2)}) copy-start(bf16[64,4096]{1,0:T(8,128)(2,1)} %copy-done.4) | copy-start | bytes 1572868
  513.6 349.8 %copy-start.6 = (bf16[64,4096]{1,0:T(8,128)(2,1)S(1)}, bf16[64,4096]{1,0:T(8,128)(2,1)}, u32[]{:S(2)}) copy-start(bf16[64,4096]{1,0:T(8,128)(2,1)} %reduce-scatter.9.cloned.1.call-done) | copy-start | bytes 1572868
Sparse Core Ops, SparseCore 0:
  9.7 33.2 all-gather.19
  45.1 70.8 all-gather.21
  118.2 70.5 all-gather.23
  190.8 44.8 all-gather.25
  237.7 44.5 all-gather.27
  287.4 28.8 reduce-scatter.6
  323.5 30.5 all-gather.13
  382.6 29.6 reduce-scatter.8
  414.6 30.5 all-gather.15
  446.7 30.8 all-gather.17
  485.7 74.6 reduce-scatter.14
  564.5 73.5 reduce-scatter.12
  642.0 84.4 reduce-scatter.16
  730.3 83.8 reduce-scatter.10
where the time goes:
time: 872 us; the launch traced here: 871 us
  waiting for transfers between devices  386 us (44%)
  blocking collectives  349 us (40%)
  matrix products  94.5 us (11%)
  local copies, waits for them, and re-layouts  17.6 us (2%)
  between operations  14.3 us (2%)
    psum x1, blocking collectives, local(): gain_total = lax.psum(gain_first + gain_second, ('tensor', 'dp'))  349 us
    all_gather x1, waiting for transfers between devices, local(): lax.all_gather(w_out[0], 'dp', axis=0, tiled=True)  73.1 us
    all_gather x2, waiting for transfers between devices, backward(): lax.all_gather(normed, 'tensor', axis=0, tiled=True)  59.7 us
    reduce_scatter x2, waiting for transfers between devices, backward(): lax.psum_scatter((total + against(value_gradient, full_value)).astype(jnp...  56.6 us
    all_gather x1, waiting for transfers between devices, local(): lax.all_gather(w_query[0], 'dp', axis=0, tiled=True)  55.6 us
    all_gather x2, waiting for transfers between devices, backward(): lax.all_gather(upstream_part, 'tensor', axis=0, tiled=True)  55.4 us
    all_gather x1, waiting for transfers between devices, local(): lax.all_gather(value_weight[0], 'dp', axis=0, tiled=True)  41 us
    all_gather x1, waiting for transfers between devices, local(): lax.all_gather(key_weight[0], 'dp', axis=0, tiled=True)  39.1 us
  transfers between devices with their start and end apart: 15, of which 11 were waited for; matrix products, arithmetic and copies ran while one was open for 8% of the time, Pallas kernels for 0%

commit v1 on v0

v1 whole, which is shorter than its diff:
```python
import functools
import math

import jax
import jax.numpy as jnp
from jax import lax
from jax.experimental import pallas as pl
from jax.experimental.pallas import tpu as pltpu
from jax.sharding import PartitionSpec as P

BF16 = jnp.bfloat16
F32 = jnp.float32
MESH = pl.DeviceIdType.MESH
HEAD = 128
EPS = 1e-05
RING = 4
TOK = 256
SUB = 64
WIDTH = 4096
GROUP = 1024
BLOCK = 256
QCOLS = 1024
KVCOLS = 256
DCOLS = QCOLS + 2 * KVCOLS
ALLCOLS = DCOLS + QCOLS
SCALE = 1.0 / math.sqrt(HEAD)
ORDER = (1, 3, 2)


def nn(left, right):
    return lax.dot_general(left, right, (((1,), (0,)), ((), ())), preferred_element_type=F32)


def nt(left, right):
    return lax.dot_general(left, right, (((1,), (1,)), ((), ())), preferred_element_type=F32)


def tn(left, right):
    return lax.dot_general(left, right, (((0,), (0,)), ((), ())), preferred_element_type=F32)


def at(index, size):
    return pl.ds(pl.multiple_of(index * size, size), size)


def kernel(
    x_ref, top_ref, q_ref, k_ref, v_ref, seg_ref, gain_ref, wq_ref, wk_ref, wv_ref, wo_ref,
    bottom_ref, gq_ref, gk_ref, gv_ref, go_ref, gg_ref,
    up_own, nm_own, up_all, nm_all, w_out, w_qkv, d_all, att_all, g_part, g_recv, g_own, probs,
    n_part, n_recv, n_sum, f_recv, pipe_src, p_part, p_recv, inv_ref, gn_own,
    gain_mine, gain_x, gain_a, gain_b,
    send_sem, up_a_sem, up_x_sem, nm_a_sem, nm_x_sem, w_sem, r_sem, d_sem, att_sem, n_sem, f_sem,
    pipe_sem, p_sem, gx_sem, ga_sem, gb_sem, local_sem,
):
    p = lax.axis_index("pipe")
    t = lax.axis_index("tensor")
    dp = lax.axis_index("dp")
    z = lax.div(dp, RING)
    y = lax.rem(dp, RING)
    a = (1 - p) * z + p * y
    b = (1 - p) * y + p * z

    def dp_of(aa, bb):
        return (1 - p) * (RING * aa + bb) + p * (RING * bb + aa)

    def plus(i, o):
        return lax.rem(i + o, RING)

    def dev_x(o):
        return (p, plus(t, o), dp)

    def dev_a(o):
        return (p, t, dp_of(plus(a, o), b))

    def dev_b(o):
        return (p, t, dp_of(a, plus(b, o)))

    dev_p = (1 - p, t, dp)

    sends = []

    def send(src, dst, recv_sem, device):
        copy = pltpu.make_async_remote_copy(
            src_ref=src, dst_ref=dst, send_sem=send_sem.at[len(sends)], recv_sem=recv_sem,
            device_id=device, device_id_type=MESH,
        )
        copy.start()
        sends.append(copy)
        return copy

    def arrived(dst, recv_sem):
        pltpu.make_async_remote_copy(
            src_ref=dst, dst_ref=dst, send_sem=send_sem.at[0], recv_sem=recv_sem,
            device_id=dev_p, device_id_type=MESH,
        ).wait_recv()

    barrier = pltpu.get_barrier_semaphore()
    partners = [f(o) for f in (dev_x, dev_a, dev_b) for o in ORDER] + [dev_p]
    for device in partners:
        pl.semaphore_signal(barrier, inc=1, device_id=device, device_id_type=MESH)

    blocks = [(i, j) for i in range(RING) for j in range(RING)]

    def cols_of(j):
        return pl.ds(j * BLOCK, BLOCK)

    own_weights = [
        pltpu.make_async_copy(wo_ref, w_out.at[at(b, BLOCK), :], local_sem.at[0]),
        pltpu.make_async_copy(wq_ref, w_qkv.at[at(b, BLOCK), pl.ds(0, QCOLS)], local_sem.at[1]),
        pltpu.make_async_copy(
            wk_ref, w_qkv.at[at(b, BLOCK), pl.ds(QCOLS, KVCOLS)], local_sem.at[2]
        ),
        pltpu.make_async_copy(
            wv_ref, w_qkv.at[at(b, BLOCK), pl.ds(QCOLS + KVCOLS, KVCOLS)], local_sem.at[3]
        ),
    ]
    for copy in own_weights:
        copy.start()

    for i, j in blocks:
        up_own[0, i, :, cols_of(j)] = top_ref[:, at(dp_of(i, j), BLOCK)]

    pl.semaphore_wait(barrier, len(partners))

    def slab(i):
        return pl.ds(pl.multiple_of(i * TOK + t * SUB, SUB), SUB)

    def spread_a(own, gathered, sem, m):
        for o in ORDER:
            send(own.at[m, plus(a, o)], gathered.at[m, slab(a), :], sem.at[m, a], dev_a(o))
        gathered[m, slab(a), :] = own[m, a]

    def spread_x(gathered, a_sem, sem, m):
        for step in (0,) + ORDER:
            i = plus(a, step)
            if step:
                arrived(gathered.at[m, slab(i), :], a_sem.at[m, i])
            for o in ORDER:
                send(
                    gathered.at[m, slab(i), :], gathered.at[m, slab(i), :], sem.at[m, i, t], dev_x(o)
                )

    def wait_x(gathered, sem, m, i):
        for o in ORDER:
            source = plus(t, o)
            rows = pl.ds(pl.multiple_of(i * TOK + source * SUB, SUB), SUB)
            arrived(gathered.at[m, rows, :], sem.at[m, i, source])

    spread_a(up_own, up_all, up_a_sem, 0)
    for o in ORDER:
        send(wo_ref, w_out.at[at(b, BLOCK), :], w_sem.at[0, b], dev_b(o))
    for o in ORDER:
        send(wq_ref, w_qkv.at[at(b, BLOCK), pl.ds(0, QCOLS)], w_sem.at[1, b], dev_b(o))
        send(wk_ref, w_qkv.at[at(b, BLOCK), pl.ds(QCOLS, KVCOLS)], w_sem.at[2, b], dev_b(o))
        send(wv_ref, w_qkv.at[at(b, BLOCK), pl.ds(QCOLS + KVCOLS, KVCOLS)], w_sem.at[3, b], dev_b(o))

    def norm(m):
        square = jnp.zeros((SUB, 1), F32)
        for f in range(16):
            x = x_ref[m, :, cols_of(f)].astype(F32)
            square = square + jnp.sum(x * x, axis=-1, keepdims=True)
        inv = lax.rsqrt(square * (1.0 / WIDTH) + EPS)
        inv_ref[m] = jnp.broadcast_to(inv, (SUB, HEAD))
        for i, j in blocks:
            feature = at(dp_of(i, j), BLOCK)
            x = x_ref[m, :, feature].astype(F32)
            nm_own[m, i, :, cols_of(j)] = (x * inv * gain_ref[:, feature]).astype(BF16)

    spread_x(up_all, up_a_sem, up_x_sem, 0)
    norm(0)
    norm(1)
    spread_a(nm_own, nm_all, nm_a_sem, 0)
    spread_a(nm_own, nm_all, nm_a_sem, 1)

    rows_own = at(a, TOK)

    def forward(m):
        seg_row = jnp.broadcast_to(seg_ref[m : m + 1, :], (TOK, TOK)).astype(F32)
        seg_col = jnp.transpose(seg_row)
        row = lax.broadcasted_iota(jnp.int32, (TOK, TOK), 0)
        col = lax.broadcasted_iota(jnp.int32, (TOK, TOK), 1)
        allowed = (row <= col) & (seg_row == seg_col)
        bias = jnp.where(allowed, 0.0, -1e30).astype(F32)

        def group(g, carry):
            key = k_ref[m, :, at(g, HEAD)]
            value = v_ref[m, :, at(g, HEAD)]
            for h in range(RING):
                cols = at(g * RING + h, HEAD)
                scores = nt(key, q_ref[m, :, cols]) * SCALE + bias
                top = jnp.max(scores, axis=0, keepdims=True)
                raised = jnp.exp(scores - top)
                attention = raised * (1.0 / jnp.sum(raised, axis=0, keepdims=True))
                probs[m, g * RING + h] = attention
                att_all[m, rows_own, cols] = tn(attention.astype(BF16), value).astype(BF16)
            return carry

        lax.fori_loop(0, 2, group, 0)

    def grad_attn_partial(m):
        def rows(i, dst):
            def chunk(n, carry):
                cols = at(n, BLOCK)
                dst[:, cols] = nn(up_all[m, at(i, TOK), :], w_out[:, cols]).astype(BF16)
                return carry

            lax.fori_loop(0, RING, chunk, 0)

        for o in ORDER:
            i = plus(a, o)
            wait_x(up_all, up_x_sem, m, i)
            rows(i, g_part.at[i])
            send(g_part.at[i], g_recv.at[m, a], r_sem.at[m, a], dev_a(o))
        wait_x(up_all, up_x_sem, m, a)
        rows(a, g_recv.at[m, a])

    def grad_attn_sum(m):
        for o in ORDER:
            arrived(g_recv.at[m, plus(a, o)], r_sem.at[m, plus(a, o)])
        for n in range(RING):
            cols = cols_of(n)
            total = g_recv[m, 0, :, cols].astype(F32)
            for i in range(1, RING):
                total = total + g_recv[m, i, :, cols].astype(F32)
            g_own[:, cols] = total.astype(BF16)

    def backward(m):
        def group(g, carry):
            key = k_ref[m, :, at(g, HEAD)]
            value = v_ref[m, :, at(g, HEAD)]
            dk = jnp.zeros((TOK, HEAD), F32)
            dv = jnp.zeros((TOK, HEAD), F32)
            for h in range(RING):
                cols = at(g * RING + h, HEAD)
                grad = g_own[:, cols]
                attention = probs[m, g * RING + h]
                grad_probs = nt(value, grad)
                row_dot = jnp.sum(attention * grad_probs, axis=0, keepdims=True)
                score = (attention * (grad_probs - row_dot) * SCALE).astype(BF16)
                d_all[m, rows_own, cols] = tn(score, key).astype(BF16)
                dk = dk + nn(score, q_ref[m, :, cols])
                dv = dv + nn(attention.astype(BF16), grad)
            d_all[m, rows_own, pl.ds(pl.multiple_of(QCOLS + g * HEAD, HEAD), HEAD)] = dk.astype(BF16)
            d_all[m, rows_own, pl.ds(pl.multiple_of(QCOLS + KVCOLS + g * HEAD, HEAD), HEAD)] = (
                dv.astype(BF16)
            )
            return carry

        lax.fori_loop(0, 2, group, 0)

    def spread_d(m):
        for o in ORDER:
            send(d_all.at[m, rows_own, :], d_all.at[m, rows_own, :], d_sem.at[m, a], dev_a(o))
        for o in ORDER:
            send(att_all.at[m, rows_own, :], att_all.at[m, rows_own, :], att_sem.at[m, a], dev_a(o))

    def grad_normed_partial(m):
        for step in (0,) + ORDER:
            i = plus(a, step)
            if step:
                arrived(d_all.at[m, at(i, TOK), :], d_sem.at[m, i])

            def chunk(n, carry):
                cols = at(n, BLOCK)
                part = nt(d_all[m, at(i, TOK), :], w_qkv[at(n, BLOCK), :]).astype(BF16)
                for u in range(RING):
                    n_part[u, i, :, cols] = part[u * SUB : (u + 1) * SUB, :]
                return carry

            lax.fori_loop(0, RING, chunk, 0)
            for o in ORDER:
                send(
                    n_part.at[plus(t, o), i], n_recv.at[m, t, i], n_sem.at[m, t, i], dev_x(o)
                )
            n_recv[m, t, i] = n_part[t, i]

    def grad_normed_sum(m):
        for step in ORDER + (0,):
            i = plus(a, step)
            for o in ORDER:
                arrived(n_recv.at[m, plus(t, o), i], n_sem.at[m, plus(t, o), i])
            for n in range(RING):
                cols = cols_of(n)
                total = n_recv[m, 0, i, :, cols].astype(F32)
                for u in range(1, RING):
                    total = total + n_recv[m, u, i, :, cols].astype(F32)
                n_sum[i, :, cols] = total.astype(BF16)
            if step:
                send(n_sum.at[i], f_recv.at[m, a], f_sem.at[m, a], dev_a(step))
        f_recv[m, a] = n_sum[a]
        for o in ORDER:
            arrived(f_recv.at[m, plus(a, o)], f_sem.at[m, plus(a, o)])

    def grad_input(m):
        inv = inv_ref[m][:, :1]
        total = jnp.zeros((SUB, 1), F32)
        for i, j in blocks:
            feature = at(dp_of(i, j), BLOCK)
            unit = x_ref[m, :, feature].astype(F32) * inv
            grad = f_recv[m, i, :, cols_of(j)].astype(F32)
            term = unit * grad
            total = total + jnp.sum(term * gain_ref[:, feature], axis=-1, keepdims=True)
            place = (pl.ds(i * 2 + j // 2, 1), cols_of(j % 2))
            gain_sum = jnp.sum(term, axis=0, keepdims=True)
            if m == 0:
                gain_mine[place] = gain_sum
            else:
                gain_mine[place] = gain_mine[place] + gain_sum
        mean = total * (1.0 / WIDTH)
        for i, j in blocks:
            feature = at(dp_of(i, j), BLOCK)
            unit = x_ref[m, :, feature].astype(F32) * inv
            grad = f_recv[m, i, :, cols_of(j)].astype(F32)
            result = up_own[m, i, :, cols_of(j)].astype(F32) + inv * (
                gain_ref[:, feature] * grad - unit * mean
            )
            if m == 0:
                pipe_src[i, :, cols_of(j)] = result.astype(BF16)
            else:
                bottom_ref[:, feature] = result.astype(BF16)

    forward(0)
    own_weights[0].wait()
    for o in ORDER:
        arrived(w_out.at[at(plus(b, o), BLOCK), :], w_sem.at[0, plus(b, o)])
    grad_attn_partial(0)
    spread_x(nm_all, nm_a_sem, nm_x_sem, 0)
    forward(1)
    grad_attn_sum(0)
    backward(0)
    spread_d(0)
    for copy in own_weights[1:]:
        copy.wait()
    for o in ORDER:
        rows = at(plus(b, o), BLOCK)
        arrived(w_qkv.at[rows, pl.ds(0, QCOLS)], w_sem.at[1, plus(b, o)])
        arrived(w_qkv.at[rows, pl.ds(QCOLS, KVCOLS)], w_sem.at[2, plus(b, o)])
        arrived(w_qkv.at[rows, pl.ds(QCOLS + KVCOLS, KVCOLS)], w_sem.at[3, plus(b, o)])
    grad_normed_partial(0)
    n_sends = sends[-12:]
    grad_normed_sum(0)
    grad_input(0)
    for i, j in blocks:
        send(
            pipe_src.at[i, :, cols_of(j)], up_own.at[1, j, :, cols_of(i)], pipe_sem.at[0], dev_p
        )
    spread_x(nm_all, nm_a_sem, nm_x_sem, 1)
    waited = []
    for copy in sends:
        copy.wait_send()
    n_done = len(sends)
    arrived(up_own.at[1], pipe_sem.at[0])

    spread_a(up_own, up_all, up_a_sem, 1)
    spread_x(up_all, up_a_sem, up_x_sem, 1)
    grad_attn_partial(1)
    grad_attn_sum(1)
    backward(1)
    spread_d(1)
    grad_normed_partial(1)

    for m in range(2):
        for i in range(RING):
            wait_x(nm_all, nm_x_sem, m, i)
    for m in range(2):
        for o in ORDER:
            if m == 0:
                pass
            arrived(att_all.at[m, at(plus(a, o), TOK), :], att_sem.at[m, plus(a, o)])

    def weight_grads(j, dst):
        feature = at(j, BLOCK)

        def chunk(n, carry):
            cols = at(n, 512)
            total = tn(nm_all[0, :, feature], d_all[0, :, cols])
            total = total + tn(nm_all[1, :, feature], d_all[1, :, cols])
            dst[:, cols] = total.astype(BF16)
            return carry

        lax.fori_loop(0, DCOLS // 512, chunk, 0)

        def chunk_out(n, carry):
            cols = at(n, 512)
            total = tn(up_all[0, :, feature], att_all[0, :, cols])
            total = total + tn(up_all[1, :, feature], att_all[1, :, cols])
            dst[:, pl.ds(pl.multiple_of(DCOLS + n * 512, 512), 512)] = total.astype(BF16)
            return carry

        lax.fori_loop(0, QCOLS // 512, chunk_out, 0)

    for o in ORDER:
        j = plus(b, o)
        weight_grads(j, p_part.at[j])
        send(p_part.at[j], p_recv.at[b], p_sem.at[b], dev_b(o))
    weight_grads(b, p_recv.at[b])

    grad_normed_sum(1)
    grad_input(1)

    gain_x[t] = gain_mine[...]
    for o in ORDER:
        send(gain_x.at[t], gain_x.at[t], gx_sem.at[t], dev_x(o))
    for o in ORDER:
        arrived(gain_x.at[plus(t, o)], gx_sem.at[plus(t, o)])
    gain_a[a] = gain_x[0] + gain_x[1] + gain_x[2] + gain_x[3]
    for o in ORDER:
        send(gain_a.at[a], gain_a.at[a], ga_sem.at[a], dev_a(o))
    for o in ORDER:
        arrived(gain_a.at[plus(a, o)], ga_sem.at[plus(a, o)])
    gain_b[b] = gain_a[0] + gain_a[1] + gain_a[2] + gain_a[3]
    for o in ORDER:
        send(gain_b.at[b], gain_b.at[b], gb_sem.at[b], dev_b(o))
    for o in ORDER:
        arrived(gain_b.at[plus(b, o)], gb_sem.at[plus(b, o)])
    gain_mine[...] = gain_b[0] + gain_b[1] + gain_b[2] + gain_b[3]
    for i, j in blocks:
        gg_ref[:, at(dp_of(i, j), BLOCK)] = gain_mine[pl.ds(i * 2 + j // 2, 1), cols_of(j % 2)]

    for o in ORDER:
        arrived(p_recv.at[plus(b, o)], p_sem.at[plus(b, o)])

    def summed(cols):
        total = p_recv[0, :, cols].astype(F32)
        for i in range(1, RING):
            total = total + p_recv[i, :, cols].astype(F32)
        return total.astype(BF16)

    for n in range(4):
        gq_ref[:, cols_of(n)] = summed(cols_of(n))
        go_ref[:, cols_of(n)] = summed(pl.ds(DCOLS + n * BLOCK, BLOCK))
    gk_ref[...] = summed(pl.ds(QCOLS, KVCOLS))
    gv_ref[...] = summed(pl.ds(QCOLS + KVCOLS, KVCOLS))
    for copy in sends[n_done:]:
        copy.wait_send()


def local(x_saved, grad_top, query, key, value, segment, w_query, key_weight, value_weight, w_out, gain):
    vmem = pl.BlockSpec(memory_space=pltpu.VMEM)
    hbm = pl.BlockSpec(memory_space=pl.ANY)
    dma = pltpu.SemaphoreType.DMA
    outs = pl.pallas_call(
        kernel,
        out_shape=(
            jax.ShapeDtypeStruct((SUB, WIDTH), BF16),
            jax.ShapeDtypeStruct((BLOCK, QCOLS), BF16),
            jax.ShapeDtypeStruct((BLOCK, KVCOLS), BF16),
            jax.ShapeDtypeStruct((BLOCK, KVCOLS), BF16),
            jax.ShapeDtypeStruct((BLOCK, QCOLS), BF16),
            jax.ShapeDtypeStruct((1, WIDTH), F32),
        ),
        in_specs=[vmem] * 7 + [hbm] * 4,
        out_specs=(vmem,) * 6,
        scratch_shapes=[
            pltpu.VMEM((2, RING, SUB, GROUP), BF16),
            pltpu.VMEM((2, RING, SUB, GROUP), BF16),
            pltpu.VMEM((2, GROUP, GROUP), BF16),
            pltpu.VMEM((2, GROUP, GROUP), BF16),
            pltpu.VMEM((GROUP, QCOLS), BF16),
            pltpu.VMEM((GROUP, DCOLS), BF16),
            pltpu.VMEM((2, GROUP, DCOLS), BF16),
            pltpu.VMEM((2, GROUP, QCOLS), BF16),
            pltpu.VMEM((RING, TOK, QCOLS), BF16),
            pltpu.VMEM((2, RING, TOK, QCOLS), BF16),
            pltpu.VMEM((TOK, QCOLS), BF16),
            pltpu.VMEM((2, 8, TOK, TOK), F32),
            pltpu.VMEM((RING, RING, SUB, GROUP), BF16),
            pltpu.VMEM((2, RING, RING, SUB, GROUP), BF16),
            pltpu.VMEM((RING, SUB, GROUP), BF16),
            pltpu.VMEM((2, RING, SUB, GROUP), BF16),
            pltpu.VMEM((RING, SUB, GROUP), BF16),
            pltpu.VMEM((RING, BLOCK, ALLCOLS), BF16),
            pltpu.VMEM((RING, BLOCK, ALLCOLS), BF16),
            pltpu.VMEM((2, SUB, HEAD), F32),
            pltpu.VMEM((8, 128), F32),
            pltpu.VMEM((8, 512), F32),
            pltpu.VMEM((RING, 8, 512), F32),
            pltpu.VMEM((RING, 8, 512), F32),
            pltpu.VMEM((RING, 8, 512), F32),
            dma((200,)),
            dma((2, RING)),
            dma((2, RING, RING)),
            dma((2, RING)),
            dma((2, RING, RING)),
            dma((RING, RING)),
            dma((2, RING)),
            dma((2, RING)),
            dma((2, RING)),
            dma((2, RING, RING)),
            dma((2, RING)),
            dma((1,)),
            dma((RING,)),
            dma((RING,)),
            dma((RING,)),
            dma((RING,)),
            dma((4,)),
        ],
        compiler_params=pltpu.CompilerParams(
            collective_id=0, has_side_effects=True, vmem_limit_bytes=63 * 2**20
        ),
        cost_estimate=pl.CostEstimate(flops=23 * 10**9, bytes_accessed=8 * 10**6, transcendentals=10**6),
        name="relay_backward",
    )(
        x_saved[0, 0], grad_top[0, 0], query[0, 0], key[0, 0], value[0, 0], segment[0, 0], gain,
        w_query[0], key_weight[0], value_weight[0], w_out[0],
    )
    bottom, gq, gk, gv, go, gg = outs
    return (bottom[None, None], gq[None], gk[None], gv[None], go[None], gg)


def solution(mesh):
    in_specs = (
        P("pipe", "dp", None, "tensor", None),
        P("pipe", "dp", "tensor", None),
        P("pipe", "dp", None, None, "tensor"),
        P("pipe", "dp", None, None, "tensor"),
        P("pipe", "dp", None, None, "tensor"),
        P("pipe", "dp", None, None),
        P("pipe", "dp", "tensor"),
        P("pipe", "dp", "tensor"),
        P("pipe", "dp", "tensor"),
        P("pipe", "dp", "tensor"),
        P("pipe", None),
    )
    out_specs = (
        P("pipe", "dp", "tensor", None),
        P("pipe", "dp", "tensor"),
        P("pipe", "dp", "tensor"),
        P("pipe", "dp", "tensor"),
        P("pipe", "dp", "tensor"),
        P("pipe", None),
    )
    return jax.shard_map(local, mesh=mesh, in_specs=in_specs, out_specs=out_specs, check_vma=False)
```

time: 872 us -> 251 us (0.29)
  waiting for transfers between devices: 386 us -> 0 us
  blocking collectives: 349 us -> 0 us
  Pallas kernels: 0 us -> 245 us
  matrix products: 94.5 us -> 0 us
  between operations: 14.3 us -> 0.66 us
  local copies, waits for them, and re-layouts: 17.6 us -> 5.94 us
    psum x1 -> x0, blocking collectives: 349 us -> none  [local(): gain_total = lax.psum(gain_first + gain_second, ('tensor', 'dp'))]
    all_gather x8 -> x0, waiting for transfers between devices: 324 us -> none  [the longest x1 73.1 us: local(): lax.all_gather(w_out[0], 'dp', axis=0, tiled=True)]
    pallas_call x0 -> x1, Pallas kernels: none -> 245 us  [local(): pl.pallas_call(kernel, out_shape=(jax.ShapeDtypeStruct((SUB, WIDTH), BF16...]
    dot_general x22 -> x0, matrix products: 89.6 us -> none  [the longest x6 27 us: against(): lax.dot_general(left, right, (((1,), (1,)), ((), ())), preferred_element_...]
    reduce_scatter x6 -> x0, waiting for transfers between devices: 56.6 us -> none  [the longest x2 56.6 us: backward(): lax.psum_scatter((total + against(value_gradient, full_value)).astype(jnp...]
  transfers between devices with their start and end apart: 15 -> 0, of which waited for: 11 -> 0; matrix products, arithmetic and copies ran while one was open for 8% -> 0% of each run, Pallas kernels for 0% -> 0%
where the time goes in v1:
time: 251 us
  Pallas kernels  245 us (98%)
  local copies, waits for them, and re-layouts  5.94 us (2%)
    pallas_call x1, Pallas kernels, local(): pl.pallas_call(kernel, out_shape=(jax.ShapeDtypeStruct((SUB, WIDTH), BF16...  245 us
    unnamed x16, local copies, waits for them, and re-layouts  5.94 us

profile of v1, /device:TPU:0, one launch (start us, length us, event | category | flops | bytes accessed | tf_op | source)
XLA Modules:
  0.0 251.1 jit_solution(8822961852920551527)
XLA Ops:
  0.6 244.5 %relay_backward.1 = (bf16[64,4096]{1,0:T(8,128)(2,1)}, bf16[256,1024]{1,0:T(8,128)(2,1)}, bf16[256,256]{1,0:T(8,128)(2,1)}, bf16[256,256]{1,0:T(8,128)(2,1)}, bf...) custom-call(bf16[2,64,4096]{2,1,0:T(8,128)(2,1)} %bitcast.20, bf16[64,4096]{1,0:T(8,128)(2,1)} %bitcast.22, ...), custom_call_target="tpu_custom_call" | custom-call | flops 23000000512 | bytes 8000000 | tf_op jit(solution)/shard_map/relay_backward/pallas_call | solution.py:442
  245.2 0.0 copy-start.1
  245.2 1.9 copy.23
  247.1 0.0 copy-done.1
  247.1 0.0 copy-start.3
  247.1 0.0 copy-start
  247.1 0.8 copy.24
  247.9 0.2 copy-done.3
  248.1 0.0 copy-start.2
  248.1 0.7 copy.25
  248.8 0.3 copy-done.2
  249.0 0.7 copy.26
  249.7 0.0 copy-done
  249.7 0.0 copy-start.4
  249.7 0.8 copy.27
  250.5 0.0 copy-done.4
  250.5 0.6 copy.28
Async XLA Ops:
  245.2 1.9 copy-start.1
  247.1 1.0 copy-start.3
  247.1 2.6 %copy-start = (bf16[256,1024]{1,0:T(8,128)(2,1)S(1)}, bf16[256,1024]{1,0:T(8,128)(2,1)}, u32[]{:S(2)}) copy-start(bf16[256,1024]{1,0:T(8,128)(2,1)} %get-tuple-element.16) | copy-start | bytes 1572868
  248.1 1.0 copy-start.2
  249.7 0.8 copy-start.4

commit v2 on v1

v2 whole, which is shorter than its diff:
```python
import functools
import math

import jax
import jax.numpy as jnp
from jax import lax
from jax.experimental import pallas as pl
from jax.experimental.pallas import tpu as pltpu
from jax.sharding import PartitionSpec as P

BF16 = jnp.bfloat16
F32 = jnp.float32
MESH = pl.DeviceIdType.MESH
HEAD = 128
EPS = 1e-05
RING = 4
TOK = 256
SUB = 64
WIDTH = 4096
GROUP = 1024
BLOCK = 256
QCOLS = 1024
KVCOLS = 256
DCOLS = QCOLS + 2 * KVCOLS
ALLCOLS = DCOLS + QCOLS
SCALE = 1.0 / math.sqrt(HEAD)
ORDER = (1, 3, 2)


def nn(left, right):
    return lax.dot_general(left, right, (((1,), (0,)), ((), ())), preferred_element_type=F32)


def nt(left, right):
    return lax.dot_general(left, right, (((1,), (1,)), ((), ())), preferred_element_type=F32)


def tn(left, right):
    return lax.dot_general(left, right, (((0,), (0,)), ((), ())), preferred_element_type=F32)


def at(index, size):
    return pl.ds(pl.multiple_of(index * size, size), size)


def kernel(
    x_hbm, top_hbm, q_hbm, k_hbm, v_hbm, seg_ref, gain_ref, wq_ref, wk_ref, wv_ref, wo_ref,
    bottom_ref, gq_ref, gk_ref, gv_ref, go_ref, gg_ref,
    x_ref, q_ref, k_ref, v_ref,
    up_own, nm_own, up_all, nm_all, w_out, w_qkv, d_all, att_all,
    g_part, g_relay, g_recv, g_own, probs,
    n_part, n_relay, n_recv, n_sum, f_recv, pipe_src, p_part, p_relay, p_recv, inv_ref,
    gain_mine, gain_x, gain_a, gain_b,
    send_sem, up_a_sem, up_x_sem, nm_a_sem, nm_x_sem, w_sem, gr_sem, g_sem, d_sem, att_sem,
    nr_sem, n_sem, f_sem, pipe_sem, pr_sem, p_sem, gx_sem, ga_sem, gb_sem, local_sem,
):
    p = lax.axis_index("pipe")
    t = lax.axis_index("tensor")
    dp = lax.axis_index("dp")
    z = lax.div(dp, RING)
    y = lax.rem(dp, RING)
    a = (1 - p) * z + p * y
    b = (1 - p) * y + p * z

    def dp_of(aa, bb):
        return (1 - p) * (RING * aa + bb) + p * (RING * bb + aa)

    def plus(i, o):
        return lax.rem(i + o, RING)

    def dev_x(o):
        return (p, plus(t, o), dp)

    def dev_a(o):
        return (p, t, dp_of(plus(a, o), b))

    def dev_b(o):
        return (p, t, dp_of(a, plus(b, o)))

    dev_p = (1 - p, t, dp)

    sends = []
    unfinished = {}

    def send(src, dst, recv_sem, device):
        copy = pltpu.make_async_remote_copy(
            src_ref=src, dst_ref=dst, send_sem=send_sem.at[len(sends)], recv_sem=recv_sem,
            device_id=device, device_id_type=MESH,
        )
        copy.start()
        sends.append(copy)
        unfinished[id(copy)] = copy
        return copy

    def finish(copies):
        for copy in copies:
            copy.wait_send()
            del unfinished[id(copy)]

    def arrived(dst, recv_sem):
        pltpu.make_async_remote_copy(
            src_ref=dst, dst_ref=dst, send_sem=send_sem.at[0], recv_sem=recv_sem,
            device_id=dev_p, device_id_type=MESH,
        ).wait_recv()

    class Gather:
        def __init__(self, view, sem, me, device):
            self.view, self.sem, self.me, self.device = view, sem, me, device

        def copy(self, owner, half, way):
            place = self.view(owner, half)
            send(place, place, self.sem(owner, half), self.device(way))

        def wait(self, owner, half):
            arrived(self.view(owner, half), self.sem(owner, half))

        def start(self):
            for half, way in ((0, 1), (1, 3), (1, 1), (0, 3)):
                self.copy(self.me, half, way)

        def forward(self):
            for half, origin, way in ((0, 3, 1), (1, 1, 3)):
                owner = plus(self.me, origin)
                self.wait(owner, half)
                self.copy(owner, half, way)

        def near(self):
            self.wait(plus(self.me, 3), 1)
            self.wait(plus(self.me, 1), 0)

        def far(self):
            self.wait(plus(self.me, 2), 0)
            self.wait(plus(self.me, 2), 1)

    class Scatter:
        def __init__(self, part, relay, recv, relay_sem, sem, me, device):
            self.part, self.relay, self.recv = part, relay, recv
            self.relay_sem, self.sem, self.me, self.device = relay_sem, sem, me, device
            self.copies = []

        def far(self):
            for half, way in ((0, 1), (1, 3)):
                self.copies.append(
                    send(self.part(plus(self.me, 2), half), self.relay(half), self.relay_sem(half),
                         self.device(way))
                )

        def direct(self, half):
            way, other = ((1, 3)[half], 1 - half)
            self.copies.append(
                send(self.part(plus(self.me, way), other), self.recv(half, other),
                     self.sem(half, other), self.device(way))
            )

        def onward(self, half):
            way = (1, 3)[half]
            arrived(self.relay(half), self.relay_sem(half))
            place = self.part(plus(self.me, way), half)
            place[...] = (place[...].astype(F32) + self.relay(half)[...].astype(F32)).astype(BF16)
            self.copies.append(
                send(place, self.recv(half, half), self.sem(half, half), self.device(way))
            )

        def wait(self):
            for way in range(2):
                for half in range(2):
                    arrived(self.recv(way, half), self.sem(way, half))

    barrier = pltpu.get_barrier_semaphore()
    partners = [f(o) for f in (dev_x, dev_a, dev_b) for o in ORDER] + [dev_p]
    for device in partners:
        pl.semaphore_signal(barrier, inc=1, device_id=device, device_id_type=MESH)

    blocks = [(i, j) for i in range(RING) for j in range(RING)]

    def cols_of(j):
        return pl.ds(j * BLOCK, BLOCK)

    for i, j in blocks:
        pltpu.make_async_copy(
            top_hbm.at[:, at(dp_of(i, j), BLOCK)], up_own.at[0, i, :, cols_of(j)], local_sem.at[0]
        ).start()
    loads = [
        pltpu.make_async_copy(x_hbm, x_ref, local_sem.at[1]),
        pltpu.make_async_copy(q_hbm, q_ref, local_sem.at[2]),
        pltpu.make_async_copy(k_hbm, k_ref, local_sem.at[3]),
        pltpu.make_async_copy(v_hbm, v_ref, local_sem.at[4]),
        pltpu.make_async_copy(wo_ref, w_out.at[at(b, BLOCK), :], local_sem.at[5]),
        pltpu.make_async_copy(wq_ref, w_qkv.at[at(b, BLOCK), pl.ds(0, QCOLS)], local_sem.at[6]),
        pltpu.make_async_copy(
            wk_ref, w_qkv.at[at(b, BLOCK), pl.ds(QCOLS, KVCOLS)], local_sem.at[7]
        ),
        pltpu.make_async_copy(
            wv_ref, w_qkv.at[at(b, BLOCK), pl.ds(QCOLS + KVCOLS, KVCOLS)], local_sem.at[8]
        ),
    ]
    for copy in loads:
        copy.start()
    pltpu.make_async_copy(up_own.at[0], up_own.at[0], local_sem.at[0]).wait()
    pl.semaphore_wait(barrier, len(partners))

    rows_own = at(a, TOK)

    def half_rows(i, half, size):
        return pl.ds(pl.multiple_of(i * size + half * (size // 2), size // 2), size // 2)

    def slab(i):
        return pl.ds(pl.multiple_of(i * TOK + t * SUB, SUB), SUB)

    def spread_a(own, gathered, sem, m):
        for o in ORDER:
            send(own.at[m, plus(a, o)], gathered.at[m, slab(a), :], sem.at[m, a], dev_a(o))
        gathered[m, slab(a), :] = own[m, a]

    def token_gathers(gathered, sem, m):
        def make(step):
            i = plus(a, step)

            def view(owner, half):
                start = i * TOK + owner * SUB + half * (SUB // 2)
                return gathered.at[m, pl.ds(pl.multiple_of(start, SUB // 2), SUB // 2), :]

            return Gather(view, lambda owner, half: sem.at[m, i, owner, half], t, dev_x)

        return {step: make(step) for step in range(RING)}

    def row_gather(ref, sem, m):
        return Gather(
            lambda owner, half: ref.at[m, half_rows(owner, half, TOK), :],
            lambda owner, half: sem.at[m, owner, half], a, dev_a,
        )

    def weight_gather(ref, cols, index):
        return Gather(
            lambda owner, half: ref.at[half_rows(owner, half, BLOCK), cols],
            lambda owner, half: w_sem.at[index, owner, half], b, dev_b,
        )

    out_gather = weight_gather(w_out, slice(None), 0)
    qkv_gather = weight_gather(w_qkv, slice(None), 1)
    up_gathers = [token_gathers(up_all, up_x_sem, m) for m in range(2)]
    nm_gathers = [token_gathers(nm_all, nm_x_sem, m) for m in range(2)]
    d_gathers = [row_gather(d_all, d_sem, m) for m in range(2)]
    att_gathers = [row_gather(att_all, att_sem, m) for m in range(2)]

    def start_x(gathers, sem, gathered, m):
        for step in (0,) + ORDER:
            i = plus(a, step)
            if step:
                arrived(gathered.at[m, slab(i), :], sem.at[m, i])
            gathers[step].start()

    def norm(m):
        square = jnp.zeros((SUB, 1), F32)
        for f in range(16):
            x = x_ref[m, :, cols_of(f)].astype(F32)
            square = square + jnp.sum(x * x, axis=-1, keepdims=True)
        inv = lax.rsqrt(square * (1.0 / WIDTH) + EPS)
        inv_ref[m] = jnp.broadcast_to(inv, (SUB, HEAD))
        for i, j in blocks:
            feature = at(dp_of(i, j), BLOCK)
            x = x_ref[m, :, feature].astype(F32)
            nm_own[m, i, :, cols_of(j)] = (x * inv * gain_ref[:, feature]).astype(BF16)

    def forward(m):
        seg_row = jnp.broadcast_to(seg_ref[m : m + 1, :], (TOK, TOK)).astype(F32)
        seg_col = jnp.transpose(seg_row)
        row = lax.broadcasted_iota(jnp.int32, (TOK, TOK), 0)
        col = lax.broadcasted_iota(jnp.int32, (TOK, TOK), 1)
        allowed = (row <= col) & (seg_row == seg_col)
        bias = jnp.where(allowed, 0.0, -1e30).astype(F32)

        def group(g, carry):
            key = k_ref[m, :, at(g, HEAD)]
            value = v_ref[m, :, at(g, HEAD)]
            for h in range(RING):
                cols = at(g * RING + h, HEAD)
                scores = nt(key, q_ref[m, :, cols]) * SCALE + bias
                top = jnp.max(scores, axis=0, keepdims=True)
                raised = jnp.exp(scores - top)
                attention = raised * (1.0 / jnp.sum(raised, axis=0, keepdims=True))
                probs[m, g * RING + h] = attention
                att_all[m, rows_own, cols] = tn(attention.astype(BF16), value).astype(BF16)
            return carry

        lax.fori_loop(0, 2, group, 0)

    def grad_attn_rows(m, i, dst):
        def chunk(n, carry):
            cols = at(n, BLOCK)
            dst[:, cols] = nn(up_all[m, at(i, TOK), :], w_out[:, cols]).astype(BF16)
            return carry

        lax.fori_loop(0, RING, chunk, 0)

    def grad_attn_scatter(m):
        return Scatter(
            lambda dest, half: g_part.at[dest, pl.ds(half * 128, 128), :],
            lambda way: g_relay.at[m, way],
            lambda way, half: g_recv.at[m, way, pl.ds(half * 128, 128), :],
            lambda way: gr_sem.at[m, way],
            lambda way, half: g_sem.at[m, way, half],
            a, dev_a,
        )

    def grad_attn_partial(m):
        scatter = grad_attn_scatter(m)
        gathers = up_gathers[m]
        for step in (2, 1, 3, 0):
            gathers[step].near()
            gathers[step].far()
            i = plus(a, step)
            grad_attn_rows(m, i, g_part.at[i])
            if step == 2:
                scatter.far()
            elif step == 1:
                scatter.direct(0)
            elif step == 3:
                scatter.direct(1)
        return scatter

    def grad_attn_sum(m, scatter):
        scatter.onward(0)
        scatter.onward(1)
        scatter.wait()
        for n in range(RING):
            cols = cols_of(n)
            total = g_part[a, :, cols].astype(F32) + g_recv[m, 0, :, cols].astype(F32)
            g_own[:, cols] = (total + g_recv[m, 1, :, cols].astype(F32)).astype(BF16)

    def backward(m):
        def group(g, carry):
            key = k_ref[m, :, at(g, HEAD)]
            value = v_ref[m, :, at(g, HEAD)]
            dk = jnp.zeros((TOK, HEAD), F32)
            dv = jnp.zeros((TOK, HEAD), F32)
            for h in range(RING):
                cols = at(g * RING + h, HEAD)
                grad = g_own[:, cols]
                attention = probs[m, g * RING + h]
                grad_probs = nt(value, grad)
                row_dot = jnp.sum(attention * grad_probs, axis=0, keepdims=True)
                score = (attention * (grad_probs - row_dot) * SCALE).astype(BF16)
                d_all[m, rows_own, cols] = tn(score, key).astype(BF16)
                dk = dk + nn(score, q_ref[m, :, cols])
                dv = dv + nn(attention.astype(BF16), grad)
            d_all[m, rows_own, pl.ds(pl.multiple_of(QCOLS + g * HEAD, HEAD), HEAD)] = dk.astype(BF16)
            d_all[m, rows_own, pl.ds(pl.multiple_of(QCOLS + KVCOLS + g * HEAD, HEAD), HEAD)] = (
                dv.astype(BF16)
            )
            return carry

        lax.fori_loop(0, 2, group, 0)

    def grad_normed_scatter(m, step):
        i = plus(a, step)
        return Scatter(
            lambda dest, half: n_part.at[dest, i, pl.ds(half * 32, 32), :],
            lambda way: n_relay.at[m, way, i],
            lambda way, half: n_recv.at[m, way, i, pl.ds(half * 32, 32), :],
            lambda way: nr_sem.at[m, way, i],
            lambda way, half: n_sem.at[m, way, i, half],
            t, dev_x,
        )

    def grad_normed_rows(m, step):
        i = plus(a, step)

        def chunk(n, carry):
            cols = at(n, BLOCK)
            part = nt(d_all[m, at(i, TOK), :], w_qkv[at(n, BLOCK), :]).astype(BF16)
            for u in range(RING):
                n_part[u, i, :, cols] = part[u * SUB : (u + 1) * SUB, :]
            return carry

        lax.fori_loop(0, RING, chunk, 0)
        scatter = grad_normed_scatter(m, step)
        scatter.far()
        scatter.direct(0)
        scatter.direct(1)
        return scatter

    def onward(scatter):
        scatter.onward(0)
        scatter.onward(1)

    def grad_normed_sum(m, step, scatter):
        i = plus(a, step)
        scatter.wait()
        for n in range(RING):
            cols = cols_of(n)
            total = n_part[t, i, :, cols].astype(F32) + n_recv[m, 0, i, :, cols].astype(F32)
            total = (total + n_recv[m, 1, i, :, cols].astype(F32)).astype(BF16)
            if step:
                n_sum[i, :, cols] = total
            else:
                f_recv[m, i, :, cols] = total
        if step:
            return [send(n_sum.at[i], f_recv.at[m, a], f_sem.at[m, a], dev_a(step))]
        return []

    def grad_normed_back(m):
        for o in ORDER:
            arrived(f_recv.at[m, plus(a, o)], f_sem.at[m, plus(a, o)])

    def grad_input(m):
        inv = inv_ref[m][:, :1]
        total = jnp.zeros((SUB, 1), F32)
        for i, j in blocks:
            feature = at(dp_of(i, j), BLOCK)
            unit = x_ref[m, :, feature].astype(F32) * inv
            grad = f_recv[m, i, :, cols_of(j)].astype(F32)
            term = unit * grad
            total = total + jnp.sum(term * gain_ref[:, feature], axis=-1, keepdims=True)
            place = (pl.ds(i * 2 + j // 2, 1), cols_of(j % 2))
            gain_sum = jnp.sum(term, axis=0, keepdims=True)
            if m == 0:
                gain_mine[place] = gain_sum
            else:
                gain_mine[place] = gain_mine[place] + gain_sum
        mean = total * (1.0 / WIDTH)
        for i, j in blocks:
            feature = at(dp_of(i, j), BLOCK)
            unit = x_ref[m, :, feature].astype(F32) * inv
            grad = f_recv[m, i, :, cols_of(j)].astype(F32)
            result = up_own[m, i, :, cols_of(j)].astype(F32) + inv * (
                gain_ref[:, feature] * grad - unit * mean
            )
            if m == 0:
                pipe_src[i, :, cols_of(j)] = result.astype(BF16)
            else:
                bottom_ref[:, feature] = result.astype(BF16)

    def weight_rows(first, gathered, grads, width, offset):
        def rows(step):
            j = plus(b, step)
            feature = at(j, BLOCK)

            def chunk(n, carry):
                cols = at(n, 512)
                total = tn(gathered[0, :, feature], grads[0, :, cols])
                total = total + tn(gathered[1, :, feature], grads[1, :, cols])
                place = pl.ds(pl.multiple_of(offset + n * 512, 512), 512)
                p_part[j, :, place] = total.astype(BF16)
                return carry

            lax.fori_loop(0, width // 512, chunk, 0)

        scatter = Scatter(
            lambda dest, half: p_part.at[dest, pl.ds(half * 128, 128), pl.ds(offset, width)],
            lambda way: p_relay.at[way, :, pl.ds(offset, width)],
            lambda way, half: p_recv.at[way, pl.ds(half * 128, 128), pl.ds(offset, width)],
            lambda way: pr_sem.at[first, way],
            lambda way, half: p_sem.at[first, way, half],
            b, dev_b,
        )
        rows(2)
        scatter.far()
        rows(1)
        scatter.direct(0)
        rows(3)
        scatter.direct(1)
        rows(0)
        return scatter

    def summed(cols):
        total = p_part[b, :, cols].astype(F32) + p_recv[0, :, cols].astype(F32)
        return (total + p_recv[1, :, cols].astype(F32)).astype(BF16)

    spread_a(up_own, up_all, up_a_sem, 0)
    loads[4].wait()
    out_gather.start()
    up_gathers[0][0].start()
    loads[0].wait()
    norm(0)
    norm(1)
    for step in ORDER:
        i = plus(a, step)
        arrived(up_all.at[0, slab(i), :], up_a_sem.at[0, i])
        up_gathers[0][step].start()
    spread_a(nm_own, nm_all, nm_a_sem, 0)
    spread_a(nm_own, nm_all, nm_a_sem, 1)
    for copy in loads[5:]:
        copy.wait()
    out_gather.forward()
    qkv_gather.start()
    for copy in loads[1:4]:
        copy.wait()
    forward(0)
    for step in (0, 2, 1, 3):
        up_gathers[0][step].forward()
    forward(1)
    att_gathers[0].start()
    out_gather.near()
    out_gather.far()
    scatter = grad_attn_partial(0)
    g_copies = scatter.copies
    qkv_gather.forward()
    start_x(nm_gathers[0], nm_a_sem, nm_all, 0)
    att_gathers[0].forward()
    grad_attn_sum(0, scatter)
    backward(0)
    d_gathers[0].start()
    qkv_gather.near()
    qkv_gather.far()
    for step in range(RING):
        nm_gathers[0][step].forward()
    n_copies = []

    def grad_normed(m):
        scatters = {0: grad_normed_rows(m, 0)}
        d_gathers[m].forward()
        if m == 0:
            att_gathers[1].start()
        d_gathers[m].near()
        onward(scatters[0])
        scatters[1] = grad_normed_rows(m, 1)
        scatters[3] = grad_normed_rows(m, 3)
        onward(scatters[1])
        d_gathers[m].far()
        scatters[2] = grad_normed_rows(m, 2)
        onward(scatters[3])
        return scatters

    def grad_normed_end(m, scatters):
        copies = []
        copies += grad_normed_sum(m, 0, scatters[0])
        copies += grad_normed_sum(m, 1, scatters[1])
        onward(scatters[2])
        copies += grad_normed_sum(m, 3, scatters[3])
        copies += grad_normed_sum(m, 2, scatters[2])
        grad_normed_back(m)
        for part in scatters.values():
            copies += part.copies
        return copies

    scatters = grad_normed(0)
    n_copies = grad_normed_end(0, scatters)
    grad_input(0)
    for i, j in blocks:
        send(
            pipe_src.at[i, :, cols_of(j)], up_own.at[1, j, :, cols_of(i)], pipe_sem.at[0], dev_p
        )
    att_gathers[1].forward()
    arrived(up_own.at[1], pipe_sem.at[0])

    spread_a(up_own, up_all, up_a_sem, 1)
    start_x(up_gathers[1], up_a_sem, up_all, 1)
    finish(g_copies)
    finish(n_copies)
    for step in (0, 2, 1, 3):
        up_gathers[1][step].forward()
    for gather in att_gathers + [nm_gathers[0][step] for step in range(RING)]:
        gather.near()
        gather.far()
    scatter = grad_attn_partial(1)
    start_x(nm_gathers[1], nm_a_sem, nm_all, 1)
    out_scatter = weight_rows(0, up_all, att_all, QCOLS, DCOLS)
    grad_attn_sum(1, scatter)
    backward(1)
    d_gathers[1].start()
    for step in range(RING):
        nm_gathers[1][step].forward()
    onward(out_scatter)
    scatters = grad_normed(1)
    for step in range(RING):
        nm_gathers[1][step].near()
        nm_gathers[1][step].far()
    qkv_scatter = weight_rows(1, nm_all, d_all, DCOLS, 0)
    grad_normed_end(1, scatters)
    onward(qkv_scatter)
    grad_input(1)

    gain_x[t] = gain_mine[...]
    for o in ORDER:
        send(gain_x.at[t], gain_x.at[t], gx_sem.at[t], dev_x(o))
    out_scatter.wait()
    for n in range(4):
        go_ref[:, cols_of(n)] = summed(pl.ds(DCOLS + n * BLOCK, BLOCK))
    for o in ORDER:
        arrived(gain_x.at[plus(t, o)], gx_sem.at[plus(t, o)])
    gain_a[a] = gain_x[0] + gain_x[1] + gain_x[2] + gain_x[3]
    for o in ORDER:
        send(gain_a.at[a], gain_a.at[a], ga_sem.at[a], dev_a(o))
    for o in ORDER:
        arrived(gain_a.at[plus(a, o)], ga_sem.at[plus(a, o)])
    gain_b[b] = gain_a[0] + gain_a[1] + gain_a[2] + gain_a[3]
    for o in ORDER:
        send(gain_b.at[b], gain_b.at[b], gb_sem.at[b], dev_b(o))
    for o in ORDER:
        arrived(gain_b.at[plus(b, o)], gb_sem.at[plus(b, o)])
    gain_mine[...] = gain_b[0] + gain_b[1] + gain_b[2] + gain_b[3]
    for i, j in blocks:
        gg_ref[:, at(dp_of(i, j), BLOCK)] = gain_mine[pl.ds(i * 2 + j // 2, 1), cols_of(j % 2)]

    qkv_scatter.wait()
    for n in range(4):
        gq_ref[:, cols_of(n)] = summed(cols_of(n))
    gk_ref[...] = summed(pl.ds(QCOLS, KVCOLS))
    gv_ref[...] = summed(pl.ds(QCOLS + KVCOLS, KVCOLS))
    finish(list(unfinished.values()))


def local(x_saved, grad_top, query, key, value, segment, w_query, key_weight, value_weight, w_out, gain):
    vmem = pl.BlockSpec(memory_space=pltpu.VMEM)
    hbm = pl.BlockSpec(memory_space=pl.ANY)
    dma = pltpu.SemaphoreType.DMA
    outs = pl.pallas_call(
        kernel,
        out_shape=(
            jax.ShapeDtypeStruct((SUB, WIDTH), BF16),
            jax.ShapeDtypeStruct((BLOCK, QCOLS), BF16),
            jax.ShapeDtypeStruct((BLOCK, KVCOLS), BF16),
            jax.ShapeDtypeStruct((BLOCK, KVCOLS), BF16),
            jax.ShapeDtypeStruct((BLOCK, QCOLS), BF16),
            jax.ShapeDtypeStruct((1, WIDTH), F32),
        ),
        in_specs=[hbm] * 5 + [vmem] * 2 + [hbm] * 4,
        out_specs=(vmem,) * 6,
        scratch_shapes=[
            pltpu.VMEM((2, SUB, WIDTH), BF16),
            pltpu.VMEM((2, TOK, QCOLS), BF16),
            pltpu.VMEM((2, TOK, KVCOLS), BF16),
            pltpu.VMEM((2, TOK, KVCOLS), BF16),
            pltpu.VMEM((2, RING, SUB, GROUP), BF16),
            pltpu.VMEM((2, RING, SUB, GROUP), BF16),
            pltpu.VMEM((2, GROUP, GROUP), BF16),
            pltpu.VMEM((2, GROUP, GROUP), BF16),
            pltpu.VMEM((GROUP, QCOLS), BF16),
            pltpu.VMEM((GROUP, DCOLS), BF16),
            pltpu.VMEM((2, GROUP, DCOLS), BF16),
            pltpu.VMEM((2, GROUP, QCOLS), BF16),
            pltpu.VMEM((RING, TOK, QCOLS), BF16),
            pltpu.VMEM((2, 2, TOK // 2, QCOLS), BF16),
            pltpu.VMEM((2, 2, TOK, QCOLS), BF16),
            pltpu.VMEM((TOK, QCOLS), BF16),
            pltpu.VMEM((2, 8, TOK, TOK), F32),
            pltpu.VMEM((RING, RING, SUB, GROUP), BF16),
            pltpu.VMEM((2, 2, RING, SUB // 2, GROUP), BF16),
            pltpu.VMEM((2, 2, RING, SUB, GROUP), BF16),
            pltpu.VMEM((RING, SUB, GROUP), BF16),
            pltpu.VMEM((2, RING, SUB, GROUP), BF16),
            pltpu.VMEM((RING, SUB, GROUP), BF16),
            pltpu.VMEM((RING, BLOCK, ALLCOLS), BF16),
            pltpu.VMEM((2, BLOCK // 2, ALLCOLS), BF16),
            pltpu.VMEM((2, BLOCK, ALLCOLS), BF16),
            pltpu.VMEM((2, SUB, HEAD), F32),
            pltpu.VMEM((8, 512), F32),
            pltpu.VMEM((RING, 8, 512), F32),
            pltpu.VMEM((RING, 8, 512), F32),
            pltpu.VMEM((RING, 8, 512), F32),
            dma((320,)),
            dma((2, RING)),
            dma((2, RING, RING, 2)),
            dma((2, RING)),
            dma((2, RING, RING, 2)),
            dma((2, RING, 2)),
            dma((2, 2)),
            dma((2, 2, 2)),
            dma((2, RING, 2)),
            dma((2, RING, 2)),
            dma((2, 2, RING)),
            dma((2, 2, RING, 2)),
            dma((2, RING)),
            dma((1,)),
            dma((2, 2)),
            dma((2, 2, 2)),
            dma((RING,)),
            dma((RING,)),
            dma((RING,)),
            dma((9,)),
        ],
        compiler_params=pltpu.CompilerParams(
            collective_id=0, has_side_effects=True, vmem_limit_bytes=63 * 2**20
        ),
        cost_estimate=pl.CostEstimate(flops=23 * 10**9, bytes_accessed=8 * 10**6, transcendentals=10**6),
        name="relay_backward",
    )(
        x_saved[0, 0], grad_top[0, 0], query[0, 0], key[0, 0], value[0, 0], segment[0, 0], gain,
        w_query[0], key_weight[0], value_weight[0], w_out[0],
    )
    bottom, gq, gk, gv, go, gg = outs
    return (bottom[None, None], gq[None], gk[None], gv[None], go[None], gg)


def solution(mesh):
    in_specs = (
        P("pipe", "dp", None, "tensor", None),
        P("pipe", "dp", "tensor", None),
        P("pipe", "dp", None, None, "tensor"),
        P("pipe", "dp", None, None, "tensor"),
        P("pipe", "dp", None, None, "tensor"),
        P("pipe", "dp", None, None),
        P("pipe", "dp", "tensor"),
        P("pipe", "dp", "tensor"),
        P("pipe", "dp", "tensor"),
        P("pipe", "dp", "tensor"),
        P("pipe", None),
    )
    out_specs = (
        P("pipe", "dp", "tensor", None),
        P("pipe", "dp", "tensor"),
        P("pipe", "dp", "tensor"),
        P("pipe", "dp", "tensor"),
        P("pipe", "dp", "tensor"),
        P("pipe", None),
    )
    return jax.shard_map(local, mesh=mesh, in_specs=in_specs, out_specs=out_specs, check_vma=False)
```

time: 251 us -> 203 us (0.81)
  Pallas kernels: 245 us -> 196 us
    pallas_call x1, Pallas kernels: 245 us -> 196 us  [local(): pl.pallas_call(kernel, out_shape=(jax.ShapeDtypeStruct((SUB, WIDTH), BF16...]
where the time goes in v2:
time: 203 us
  Pallas kernels  196 us (97%)
  local copies, waits for them, and re-layouts  5.94 us (3%)
    pallas_call x1, Pallas kernels, local(): pl.pallas_call(kernel, out_shape=(jax.ShapeDtypeStruct((SUB, WIDTH), BF16...  196 us
    unnamed x16, local copies, waits for them, and re-layouts  5.94 us

profile of v2, /device:TPU:0, one launch (start us, length us, event | category | flops | bytes accessed | tf_op | source)
XLA Modules:
  0.0 202.9 jit_solution(5818754268672917700)
XLA Ops:
  0.6 196.3 %relay_backward.1 = (bf16[64,4096]{1,0:T(8,128)(2,1)}, bf16[256,1024]{1,0:T(8,128)(2,1)}, bf16[256,256]{1,0:T(8,128)(2,1)}, bf16[256,256]{1,0:T(8,128)(2,1)}, bf...) custom-call(bf16[2,64,4096]{2,1,0:T(8,128)(2,1)} %bitcast.20, bf16[64,4096]{1,0:T(8,128)(2,1)} %bitcast.22, ...), custom_call_target="tpu_custom_call" | custom-call | flops 23000000512 | bytes 8000000 | tf_op jit(solution)/shard_map/relay_backward/pallas_call | solution.py:608
  196.9 0.0 copy-start.1
  196.9 1.9 copy.23
  198.9 0.0 copy-done.1
  198.9 0.0 copy-start.3
  198.9 0.0 copy-start
  198.9 0.8 copy.24
  199.7 0.2 copy-done.3
  199.9 0.0 copy-start.2
  199.9 0.7 copy.25
  200.5 0.3 copy-done.2
  200.8 0.7 copy.26
  201.5 0.0 copy-done
  201.5 0.0 copy-start.4
  201.5 0.8 copy.27
  202.3 0.0 copy-done.4
  202.3 0.6 copy.28
Async XLA Ops:
  196.9 1.9 copy-start.1
  198.9 1.0 copy-start.3
  198.9 2.6 %copy-start = (bf16[256,1024]{1,0:T(8,128)(2,1)S(1)}, bf16[256,1024]{1,0:T(8,128)(2,1)}, u32[]{:S(2)}) copy-start(bf16[256,1024]{1,0:T(8,128)(2,1)} %get-tuple-element.16) | copy-start | bytes 1572868
  199.9 1.0 copy-start.2
  201.5 0.8 copy-start.4

commit v3 on v2

--- a/solution.py
+++ b/solution.py
@@ -25,6 +25,7 @@
 ALLCOLS = DCOLS + QCOLS
 SCALE = 1.0 / math.sqrt(HEAD)
 ORDER = (1, 3, 2)
+PART = 32
 
 
 def nn(left, right):
@@ -49,10 +50,10 @@
     x_ref, q_ref, k_ref, v_ref,
     up_own, nm_own, up_all, nm_all, w_out, w_qkv, d_all, att_all,
     g_part, g_relay, g_recv, g_own, probs,
-    n_part, n_relay, n_recv, n_sum, f_recv, pipe_src, p_part, p_relay, p_recv, inv_ref,
+    n_part, n_relay, n_recv, n_far, n_sum, f_recv, pipe_src, p_early, p_part, p_relay, p_recv, inv_ref,
     gain_mine, gain_x, gain_a, gain_b,
     send_sem, up_a_sem, up_x_sem, nm_a_sem, nm_x_sem, w_sem, gr_sem, g_sem, d_sem, att_sem,
-    nr_sem, n_sem, f_sem, pipe_sem, pr_sem, p_sem, gx_sem, ga_sem, gb_sem, local_sem,
+    nr_sem, n_sem, nf_sem, f_sem, pipe_sem, pr_sem, p_sem, gx_sem, ga_sem, gb_sem, local_sem,
 ):
     p = lax.axis_index("pipe")
     t = lax.axis_index("tensor")
@@ -168,6 +169,7 @@
 
     barrier = pltpu.get_barrier_semaphore()
     partners = [f(o) for f in (dev_x, dev_a, dev_b) for o in ORDER] + [dev_p]
+    partners += [(1 - p, t, dp_of(plus(a, o), b)) for o in ORDER]
     for device in partners:
         pl.semaphore_signal(barrier, inc=1, device_id=device, device_id_type=MESH)
 
@@ -207,22 +209,48 @@
     def slab(i):
         return pl.ds(pl.multiple_of(i * TOK + t * SUB, SUB), SUB)
 
-    def spread_a(own, gathered, sem, m):
+    def part_rows(i, owner, h):
+        return pl.ds(pl.multiple_of(i * TOK + owner * SUB + h * PART, PART), PART)
+
+    def own_part(h):
+        return pl.ds(h * PART, PART)
+
+    def spread_nm(m):
         for o in ORDER:
-            send(own.at[m, plus(a, o)], gathered.at[m, slab(a), :], sem.at[m, a], dev_a(o))
-        gathered[m, slab(a), :] = own[m, a]
-
-    def token_gathers(gathered, sem, m):
-        def make(step):
-            i = plus(a, step)
-
-            def view(owner, half):
-                start = i * TOK + owner * SUB + half * (SUB // 2)
-                return gathered.at[m, pl.ds(pl.multiple_of(start, SUB // 2), SUB // 2), :]
-
-            return Gather(view, lambda owner, half: sem.at[m, i, owner, half], t, dev_x)
-
-        return {step: make(step) for step in range(RING)}
+            send(nm_own.at[m, plus(a, o)], nm_all.at[m, slab(a), :], nm_a_sem.at[m, a], dev_a(o))
+        nm_all[m, slab(a), :] = nm_own[m, a]
+
+    def spread_up(h):
+        for o in ORDER:
+            send(
+                up_own.at[0, plus(a, o), own_part(h), :], up_all.at[0, part_rows(a, t, h), :],
+                up_a_sem.at[0, a, h], dev_a(o),
+            )
+        up_all[0, part_rows(a, t, h), :] = up_own[0, a, own_part(h), :]
+
+    def up_gather(m, step, h):
+        i = plus(a, step)
+
+        def view(owner, half):
+            start = i * TOK + owner * SUB + h * PART + half * (PART // 2)
+            return up_all.at[m, pl.ds(pl.multiple_of(start, PART // 2), PART // 2), :]
+
+        return Gather(view, lambda owner, half: up_x_sem.at[m, i, h, owner, half], t, dev_x)
+
+    def nm_gather(m, step):
+        i = plus(a, step)
+
+        def view(owner, half):
+            start = i * TOK + owner * SUB + half * (SUB // 2)
+            return nm_all.at[m, pl.ds(pl.multiple_of(start, SUB // 2), SUB // 2), :]
+
+        return Gather(view, lambda owner, half: nm_x_sem.at[m, i, owner, half], t, dev_x)
+
+    def d_gather(m, h):
+        return Gather(
+            lambda owner, half: d_all.at[m, owner, pl.ds(2 * half, 2), h],
+            lambda owner, half: d_sem.at[m, h, owner, half], a, dev_a,
+        )
 
     def row_gather(ref, sem, m):
         return Gather(
@@ -238,17 +266,19 @@
 
     out_gather = weight_gather(w_out, slice(None), 0)
     qkv_gather = weight_gather(w_qkv, slice(None), 1)
-    up_gathers = [token_gathers(up_all, up_x_sem, m) for m in range(2)]
-    nm_gathers = [token_gathers(nm_all, nm_x_sem, m) for m in range(2)]
-    d_gathers = [row_gather(d_all, d_sem, m) for m in range(2)]
+    up_gathers = [
+        {(step, h): up_gather(m, step, h) for step in range(RING) for h in range(2)}
+        for m in range(2)
+    ]
+    nm_gathers = [[nm_gather(m, step) for step in range(RING)] for m in range(2)]
+    d_gathers = [[d_gather(m, h) for h in range(2)] for m in range(2)]
     att_gathers = [row_gather(att_all, att_sem, m) for m in range(2)]
 
-    def start_x(gathers, sem, gathered, m):
-        for step in (0,) + ORDER:
-            i = plus(a, step)
-            if step:
-                arrived(gathered.at[m, slab(i), :], sem.at[m, i])
-            gathers[step].start()
+    def nm_start(m, step):
+        i = plus(a, step)
+        if step:
+            arrived(nm_all.at[m, slab(i), :], nm_a_sem.at[m, i])
+        nm_gathers[m][step].start()
 
     def norm(m):
         square = jnp.zeros((SUB, 1), F32)
@@ -296,39 +326,56 @@
     def grad_attn_scatter(m):
         return Scatter(
             lambda dest, half: g_part.at[dest, pl.ds(half * 128, 128), :],
-            lambda way: g_relay.at[m, way],
-            lambda way, half: g_recv.at[m, way, pl.ds(half * 128, 128), :],
+            lambda way: g_relay.at[way],
+            lambda way, half: g_recv.at[way, pl.ds(half * 128, 128), :],
             lambda way: gr_sem.at[m, way],
             lambda way, half: g_sem.at[m, way, half],
             a, dev_a,
         )
 
+    UNITS = ((0, 0), (1, 0), (3, 0), (2, 0), (2, 1), (1, 1), (3, 1), (0, 1))
+
+    def up_start(m, units):
+        for step, h in units:
+            i = plus(a, step)
+            if m or step:
+                arrived(up_all.at[m, part_rows(i, t, h), :], up_a_sem.at[m, i, h])
+            up_gathers[m][step, h].start()
+
+    def up_forward(m, units):
+        for unit in units:
+            up_gathers[m][unit].forward()
+
     def grad_attn_partial(m):
         scatter = grad_attn_scatter(m)
-        gathers = up_gathers[m]
-        for step in (2, 1, 3, 0):
-            gathers[step].near()
-            gathers[step].far()
+
+        def rows(step):
+            for h in range(2):
+                up_gathers[m][step, h].near()
+                up_gathers[m][step, h].far()
             i = plus(a, step)
             grad_attn_rows(m, i, g_part.at[i])
-            if step == 2:
-                scatter.far()
-            elif step == 1:
-                scatter.direct(0)
-            elif step == 3:
-                scatter.direct(1)
+
+        rows(2)
+        scatter.far()
+        rows(1)
+        scatter.direct(0)
+        rows(3)
+        scatter.direct(1)
+        rows(0)
         return scatter
 
     def grad_attn_sum(m, scatter):
-        scatter.onward(0)
-        scatter.onward(1)
         scatter.wait()
         for n in range(RING):
             cols = cols_of(n)
-            total = g_part[a, :, cols].astype(F32) + g_recv[m, 0, :, cols].astype(F32)
-            g_own[:, cols] = (total + g_recv[m, 1, :, cols].astype(F32)).astype(BF16)
+            total = g_part[a, :, cols].astype(F32) + g_recv[0, :, cols].astype(F32)
+            g_own[:, cols] = (total + g_recv[1, :, cols].astype(F32)).astype(BF16)
 
     def backward(m):
+        def put(cols, value):
+            d_all[m, a, :, :, :, cols] = value.astype(BF16).reshape(RING, 2, PART, HEAD)
+
         def group(g, carry):
             key = k_ref[m, :, at(g, HEAD)]
             value = v_ref[m, :, at(g, HEAD)]
@@ -341,40 +388,44 @@
                 grad_probs = nt(value, grad)
                 row_dot = jnp.sum(attention * grad_probs, axis=0, keepdims=True)
                 score = (attention * (grad_probs - row_dot) * SCALE).astype(BF16)
-                d_all[m, rows_own, cols] = tn(score, key).astype(BF16)
+                put(cols, tn(score, key))
                 dk = dk + nn(score, q_ref[m, :, cols])
                 dv = dv + nn(attention.astype(BF16), grad)
-            d_all[m, rows_own, pl.ds(pl.multiple_of(QCOLS + g * HEAD, HEAD), HEAD)] = dk.astype(BF16)
-            d_all[m, rows_own, pl.ds(pl.multiple_of(QCOLS + KVCOLS + g * HEAD, HEAD), HEAD)] = (
-                dv.astype(BF16)
-            )
+            put(pl.ds(pl.multiple_of(QCOLS + g * HEAD, HEAD), HEAD), dk)
+            put(pl.ds(pl.multiple_of(QCOLS + KVCOLS + g * HEAD, HEAD), HEAD), dv)
             return carry
 
         lax.fori_loop(0, 2, group, 0)
 
-    def grad_normed_scatter(m, step):
+    def grad_normed_rows(m, step, h):
         i = plus(a, step)
-        return Scatter(
-            lambda dest, half: n_part.at[dest, i, pl.ds(half * 32, 32), :],
-            lambda way: n_relay.at[m, way, i],
-            lambda way, half: n_recv.at[m, way, i, pl.ds(half * 32, 32), :],
-            lambda way: nr_sem.at[m, way, i],
-            lambda way, half: n_sem.at[m, way, i, half],
+
+        def chunk(n, carry):
+            cols = at(n, BLOCK)
+            left = d_all[m, i, :, h].reshape(RING * PART, DCOLS)
+            part = nt(left, w_qkv[at(n, BLOCK), :]).astype(BF16)
+            for u in range(RING):
+                n_part[u, i, h, :, cols] = part[u * PART : (u + 1) * PART, :]
+            return carry
+
+        lax.fori_loop(0, RING, chunk, 0)
+        if step == 2:
+            copies = [
+                send(n_part.at[plus(t, 2), i, h], n_far.at[m, h], nf_sem.at[m, h], dev_x(2)),
+                send(n_part.at[plus(t, 1), i, h], n_recv.at[m, 0, i, h], n_sem.at[m, 0, i, h, 0], dev_x(1)),
+                send(n_part.at[plus(t, 3), i, h], n_recv.at[m, 1, i, h], n_sem.at[m, 1, i, h, 0], dev_x(3)),
+            ]
+            n_copies.extend(copies)
+            return None
+        scatter = Scatter(
+            lambda dest, half: n_part.at[dest, i, h, pl.ds(half * 16, 16), :],
+            lambda way: n_relay.at[m, way, i, h],
+            lambda way, half: n_recv.at[m, way, i, h, pl.ds(half * 16, 16), :],
+            lambda way: nr_sem.at[m, way, i, h],
+            lambda way, half: n_sem.at[m, way, i, h, half],
             t, dev_x,
         )
-
-    def grad_normed_rows(m, step):
-        i = plus(a, step)
-
-        def chunk(n, carry):
-            cols = at(n, BLOCK)
-            part = nt(d_all[m, at(i, TOK), :], w_qkv[at(n, BLOCK), :]).astype(BF16)
-            for u in range(RING):
-                n_part[u, i, :, cols] = part[u * SUB : (u + 1) * SUB, :]
-            return carry
-
-        lax.fori_loop(0, RING, chunk, 0)
-        scatter = grad_normed_scatter(m, step)
+        scatter.copies = n_copies
         scatter.far()
         scatter.direct(0)
         scatter.direct(1)
@@ -384,69 +435,74 @@
         scatter.onward(0)
         scatter.onward(1)
 
-    def grad_normed_sum(m, step, scatter):
+    def grad_normed_sum(m, step, h, scatter):
         i = plus(a, step)
-        scatter.wait()
+        if step == 2:
+            arrived(n_recv.at[m, 0, i, h], n_sem.at[m, 0, i, h, 0])
+            arrived(n_recv.at[m, 1, i, h], n_sem.at[m, 1, i, h, 0])
+            arrived(n_far.at[m, h], nf_sem.at[m, h])
+        else:
+            scatter.wait()
         for n in range(RING):
             cols = cols_of(n)
-            total = n_part[t, i, :, cols].astype(F32) + n_recv[m, 0, i, :, cols].astype(F32)
-            total = (total + n_recv[m, 1, i, :, cols].astype(F32)).astype(BF16)
+            total = n_part[t, i, h, :, cols].astype(F32) + n_recv[m, 0, i, h, :, cols].astype(F32)
+            total = total + n_recv[m, 1, i, h, :, cols].astype(F32)
+            if step == 2:
+                total = total + n_far[m, h, :, cols].astype(F32)
             if step:
-                n_sum[i, :, cols] = total
+                n_sum[i, h, :, cols] = total.astype(BF16)
             else:
-                f_recv[m, i, :, cols] = total
+                f_recv[m, i, h, :, cols] = total.astype(BF16)
         if step:
-            return [send(n_sum.at[i], f_recv.at[m, a], f_sem.at[m, a], dev_a(step))]
-        return []
-
-    def grad_normed_back(m):
+            n_copies.append(
+                send(n_sum.at[i, h], f_recv.at[m, a, h], f_sem.at[m, a, h], dev_a(step))
+            )
+
+    def grad_normed_back(m, h):
         for o in ORDER:
-            arrived(f_recv.at[m, plus(a, o)], f_sem.at[m, plus(a, o)])
-
-    def grad_input(m):
-        inv = inv_ref[m][:, :1]
-        total = jnp.zeros((SUB, 1), F32)
+            arrived(f_recv.at[m, plus(a, o), h], f_sem.at[m, plus(a, o), h])
+
+    def grad_input(m, h):
+        rows = own_part(h)
+        inv = inv_ref[m, rows, :][:, :1]
+        total = jnp.zeros((PART, 1), F32)
         for i, j in blocks:
             feature = at(dp_of(i, j), BLOCK)
-            unit = x_ref[m, :, feature].astype(F32) * inv
-            grad = f_recv[m, i, :, cols_of(j)].astype(F32)
+            unit = x_ref[m, rows, feature].astype(F32) * inv
+            grad = f_recv[m, i, h, :, cols_of(j)].astype(F32)
             term = unit * grad
             total = total + jnp.sum(term * gain_ref[:, feature], axis=-1, keepdims=True)
             place = (pl.ds(i * 2 + j // 2, 1), cols_of(j % 2))
             gain_sum = jnp.sum(term, axis=0, keepdims=True)
-            if m == 0:
+            if m == 0 and h == 0:
                 gain_mine[place] = gain_sum
             else:
                 gain_mine[place] = gain_mine[place] + gain_sum
         mean = total * (1.0 / WIDTH)
         for i, j in blocks:
             feature = at(dp_of(i, j), BLOCK)
-            unit = x_ref[m, :, feature].astype(F32) * inv
-            grad = f_recv[m, i, :, cols_of(j)].astype(F32)
-            result = up_own[m, i, :, cols_of(j)].astype(F32) + inv * (
+            unit = x_ref[m, rows, feature].astype(F32) * inv
+            grad = f_recv[m, i, h, :, cols_of(j)].astype(F32)
+            result = up_own[m, i, rows, cols_of(j)].astype(F32) + inv * (
                 gain_ref[:, feature] * grad - unit * mean
             )
             if m == 0:
-                pipe_src[i, :, cols_of(j)] = result.astype(BF16)
+                pipe_src[j, rows, cols_of(i)] = result.astype(BF16)
             else:
-                bottom_ref[:, feature] = result.astype(BF16)
-
-    def weight_rows(first, gathered, grads, width, offset):
-        def rows(step):
-            j = plus(b, step)
-            feature = at(j, BLOCK)
-
-            def chunk(n, carry):
-                cols = at(n, 512)
-                total = tn(gathered[0, :, feature], grads[0, :, cols])
-                total = total + tn(gathered[1, :, feature], grads[1, :, cols])
-                place = pl.ds(pl.multiple_of(offset + n * 512, 512), 512)
-                p_part[j, :, place] = total.astype(BF16)
-                return carry
-
-            lax.fori_loop(0, width // 512, chunk, 0)
-
-        scatter = Scatter(
+                bottom_ref[rows, feature] = result.astype(BF16)
+
+    def hand_down(h):
+        rows = own_part(h)
+        for o in (0,) + ORDER:
+            j = plus(b, o)
+            send(
+                pipe_src.at[j, rows, :], up_all.at[1, part_rows(b, t, h), :],
+                up_a_sem.at[1, b, h], (1 - p, t, dp_of(a, j)),
+            )
+        send(pipe_src.at[:, rows, :], up_own.at[1, :, rows, :], pipe_sem.at[h], dev_p)
+
+    def weight_scatter(first, offset, width):
+        return Scatter(
             lambda dest, half: p_part.at[dest, pl.ds(half * 128, 128), pl.ds(offset, width)],
             lambda way: p_relay.at[way, :, pl.ds(offset, width)],
             lambda way, half: p_recv.at[way, pl.ds(half * 128, 128), pl.ds(offset, width)],
@@ -454,122 +510,172 @@
             lambda way, half: p_sem.at[first, way, half],
             b, dev_b,
         )
-        rows(2)
-        scatter.far()
-        rows(1)
-        scatter.direct(0)
-        rows(3)
-        scatter.direct(1)
-        rows(0)
-        return scatter
+
+    def out_rows(step):
+        j = plus(b, step)
+        feature = at(j, BLOCK)
+
+        def chunk(n, carry):
+            cols = at(n, 512)
+            total = tn(up_all[0, :, feature], att_all[0, :, cols])
+            total = total + tn(up_all[1, :, feature], att_all[1, :, cols])
+            place = pl.ds(pl.multiple_of(DCOLS + n * 512, 512), 512)
+            p_part[j, :, place] = total.astype(BF16)
+            return carry
+
+        lax.fori_loop(0, QCOLS // 512, chunk, 0)
+
+    def qkv_rows(m, step):
+        j = plus(b, step)
+        feature = at(j, BLOCK)
+
+        def chunk(n, carry):
+            cols = at(n, 512)
+            total = tn(nm_all[m, :, feature], d_all[m, :, :, :, :, cols].reshape(GROUP, 512))
+            if m == 0:
+                p_early[j, :, cols] = total
+            else:
+                p_part[j, :, cols] = (p_early[j, :, cols] + total).astype(BF16)
+            return carry
+
+        lax.fori_loop(0, DCOLS // 512, chunk, 0)
 
     def summed(cols):
         total = p_part[b, :, cols].astype(F32) + p_recv[0, :, cols].astype(F32)
         return (total + p_recv[1, :, cols].astype(F32)).astype(BF16)
 
-    spread_a(up_own, up_all, up_a_sem, 0)
+    n_copies = []
+    out_scatter = weight_scatter(0, DCOLS, QCOLS)
+    qkv_scatter = weight_scatter(1, 0, DCOLS)
+
+    spread_up(0)
+    spread_up(1)
+    up_start(0, UNITS[:1])
     loads[4].wait()
     out_gather.start()
-    up_gathers[0][0].start()
     loads[0].wait()
     norm(0)
-    norm(1)
-    for step in ORDER:
-        i = plus(a, step)
-        arrived(up_all.at[0, slab(i), :], up_a_sem.at[0, i])
-        up_gathers[0][step].start()
-    spread_a(nm_own, nm_all, nm_a_sem, 0)
-    spread_a(nm_own, nm_all, nm_a_sem, 1)
+    up_start(0, UNITS[1:])
+    for copy in loads[1:4]:
+        copy.wait()
+    forward(0)
+    att_gathers[0].start()
+    spread_nm(0)
     for copy in loads[5:]:
         copy.wait()
     out_gather.forward()
     qkv_gather.start()
-    for copy in loads[1:4]:
-        copy.wait()
-    forward(0)
-    for step in (0, 2, 1, 3):
-        up_gathers[0][step].forward()
+    up_forward(0, UNITS[:4])
+    norm(1)
+    spread_nm(1)
     forward(1)
-    att_gathers[0].start()
+    up_forward(0, UNITS[4:])
+    att_gathers[0].forward()
     out_gather.near()
     out_gather.far()
     scatter = grad_attn_partial(0)
     g_copies = scatter.copies
+    for step in (0, 1, 3, 2):
+        nm_start(0, step)
+    onward(scatter)
     qkv_gather.forward()
-    start_x(nm_gathers[0], nm_a_sem, nm_all, 0)
-    att_gathers[0].forward()
     grad_attn_sum(0, scatter)
     backward(0)
-    d_gathers[0].start()
-    qkv_gather.near()
-    qkv_gather.far()
-    for step in range(RING):
-        nm_gathers[0][step].forward()
-    n_copies = []
 
     def grad_normed(m):
-        scatters = {0: grad_normed_rows(m, 0)}
-        d_gathers[m].forward()
+        first, second = d_gathers[m]
+        first.start()
+        second.start()
         if m == 0:
-            att_gathers[1].start()
-        d_gathers[m].near()
-        onward(scatters[0])
-        scatters[1] = grad_normed_rows(m, 1)
-        scatters[3] = grad_normed_rows(m, 3)
-        onward(scatters[1])
-        d_gathers[m].far()
-        scatters[2] = grad_normed_rows(m, 2)
-        onward(scatters[3])
-        return scatters
-
-    def grad_normed_end(m, scatters):
-        copies = []
-        copies += grad_normed_sum(m, 0, scatters[0])
-        copies += grad_normed_sum(m, 1, scatters[1])
-        onward(scatters[2])
-        copies += grad_normed_sum(m, 3, scatters[3])
-        copies += grad_normed_sum(m, 2, scatters[2])
-        grad_normed_back(m)
-        for part in scatters.values():
-            copies += part.copies
-        return copies
-
-    scatters = grad_normed(0)
-    n_copies = grad_normed_end(0, scatters)
-    grad_input(0)
-    for i, j in blocks:
-        send(
-            pipe_src.at[i, :, cols_of(j)], up_own.at[1, j, :, cols_of(i)], pipe_sem.at[0], dev_p
-        )
-    att_gathers[1].forward()
-    arrived(up_own.at[1], pipe_sem.at[0])
-
-    spread_a(up_own, up_all, up_a_sem, 1)
-    start_x(up_gathers[1], up_a_sem, up_all, 1)
-    finish(g_copies)
-    finish(n_copies)
-    for step in (0, 2, 1, 3):
-        up_gathers[1][step].forward()
-    for gather in att_gathers + [nm_gathers[0][step] for step in range(RING)]:
+            qkv_gather.near()
+            qkv_gather.far()
+        parts = {(0, 0): grad_normed_rows(m, 0, 0), (0, 1): grad_normed_rows(m, 0, 1)}
+        first.forward()
+        for step in (0, 1, 3, 2):
+            nm_gathers[m][step].forward()
+        first.near()
+        parts[1, 0] = grad_normed_rows(m, 1, 0)
+        parts[3, 0] = grad_normed_rows(m, 3, 0)
+        onward(parts[0, 0])
+        onward(parts[0, 1])
+        second.forward()
+        first.far()
+        parts[2, 0] = grad_normed_rows(m, 2, 0)
+        onward(parts[1, 0])
+        onward(parts[3, 0])
+        second.near()
+        parts[1, 1] = grad_normed_rows(m, 1, 1)
+        parts[3, 1] = grad_normed_rows(m, 3, 1)
+        for step in (0, 1, 3, 2):
+            grad_normed_sum(m, step, 0, parts[step, 0])
+        second.far()
+        parts[2, 1] = grad_normed_rows(m, 2, 1)
+        onward(parts[1, 1])
+        onward(parts[3, 1])
+        return parts
+
+    parts = grad_normed(0)
+    grad_normed_back(0, 0)
+    grad_input(0, 0)
+    hand_down(0)
+    for step in (0, 1, 3, 2):
+        grad_normed_sum(0, step, 1, parts[step, 1])
+    up_start(1, UNITS[:4])
+    for gather in nm_gathers[0]:
         gather.near()
         gather.far()
+    qkv_rows(0, 2)
+    qkv_rows(0, 1)
+    grad_normed_back(0, 1)
+    grad_input(0, 1)
+    hand_down(1)
+    up_forward(1, UNITS[:4])
+    att_gathers[1].start()
+    qkv_rows(0, 3)
+    qkv_rows(0, 0)
+
+    up_start(1, UNITS[4:])
+    up_forward(1, UNITS[4:])
+    att_gathers[1].forward()
+    finish(g_copies)
     scatter = grad_attn_partial(1)
-    start_x(nm_gathers[1], nm_a_sem, nm_all, 1)
-    out_scatter = weight_rows(0, up_all, att_all, QCOLS, DCOLS)
+    for step in (0, 1, 3, 2):
+        nm_start(1, step)
+    onward(scatter)
+    for gather in att_gathers:
+        gather.near()
+        gather.far()
+    out_rows(2)
+    out_scatter.far()
+    out_rows(1)
+    out_scatter.direct(0)
+    out_rows(3)
+    out_scatter.direct(1)
     grad_attn_sum(1, scatter)
     backward(1)
-    d_gathers[1].start()
-    for step in range(RING):
-        nm_gathers[1][step].forward()
+    finish(n_copies)
+    parts = grad_normed(1)
     onward(out_scatter)
-    scatters = grad_normed(1)
-    for step in range(RING):
-        nm_gathers[1][step].near()
-        nm_gathers[1][step].far()
-    qkv_scatter = weight_rows(1, nm_all, d_all, DCOLS, 0)
-    grad_normed_end(1, scatters)
+    for gather in nm_gathers[1]:
+        gather.near()
+        gather.far()
+    qkv_rows(1, 2)
+    qkv_scatter.far()
+    qkv_rows(1, 1)
+    qkv_scatter.direct(0)
+    qkv_rows(1, 3)
+    qkv_scatter.direct(1)
+    for h in range(2):
+        arrived(up_own.at[1, :, own_part(h), :], pipe_sem.at[h])
+    grad_normed_back(1, 0)
+    grad_input(1, 0)
+    for step in (0, 1, 3, 2):
+        grad_normed_sum(1, step, 1, parts[step, 1])
     onward(qkv_scatter)
-    grad_input(1)
+    out_rows(0)
+    qkv_rows(1, 0)
+    grad_normed_back(1, 1)
+    grad_input(1, 1)
 
     gain_x[t] = gain_mine[...]
     for o in ORDER:
@@ -599,6 +705,11 @@
     gk_ref[...] = summed(pl.ds(QCOLS, KVCOLS))
     gv_ref[...] = summed(pl.ds(QCOLS + KVCOLS, KVCOLS))
     finish(list(unfinished.values()))
+
+
+def hand_out(*refs):
+    for src, dst in zip(refs[:6], refs[6:]):
+        dst[...] = src[...]
 
 
 def local(x_saved, grad_top, query, key, value, segment, w_query, key_weight, value_weight, w_out, gain):
@@ -628,19 +739,21 @@
             pltpu.VMEM((2, GROUP, GROUP), BF16),
             pltpu.VMEM((GROUP, QCOLS), BF16),
             pltpu.VMEM((GROUP, DCOLS), BF16),
-            pltpu.VMEM((2, GROUP, DCOLS), BF16),
+            pltpu.VMEM((2, RING, RING, 2, PART, DCOLS), BF16),
             pltpu.VMEM((2, GROUP, QCOLS), BF16),
             pltpu.VMEM((RING, TOK, QCOLS), BF16),
-            pltpu.VMEM((2, 2, TOK // 2, QCOLS), BF16),
-            pltpu.VMEM((2, 2, TOK, QCOLS), BF16),
+            pltpu.VMEM((2, TOK // 2, QCOLS), BF16),
+            pltpu.VMEM((2, TOK, QCOLS), BF16),
             pltpu.VMEM((TOK, QCOLS), BF16),
             pltpu.VMEM((2, 8, TOK, TOK), F32),
-            pltpu.VMEM((RING, RING, SUB, GROUP), BF16),
-            pltpu.VMEM((2, 2, RING, SUB // 2, GROUP), BF16),
-            pltpu.VMEM((2, 2, RING, SUB, GROUP), BF16),
+            pltpu.VMEM((RING, RING, 2, PART, GROUP), BF16),
+            pltpu.VMEM((2, 2, RING, 2, PART // 2, GROUP), BF16),
+            pltpu.VMEM((2, 2, RING, 2, PART, GROUP), BF16),
+            pltpu.VMEM((2, 2, PART, GROUP), BF16),
+            pltpu.VMEM((RING, 2, PART, GROUP), BF16),
+            pltpu.VMEM((2, RING, 2, PART, GROUP), BF16),
             pltpu.VMEM((RING, SUB, GROUP), BF16),
-            pltpu.VMEM((2, RING, SUB, GROUP), BF16),
-            pltpu.VMEM((RING, SUB, GROUP), BF16),
+            pltpu.VMEM((RING, BLOCK, DCOLS), F32),
             pltpu.VMEM((RING, BLOCK, ALLCOLS), BF16),
             pltpu.VMEM((2, BLOCK // 2, ALLCOLS), BF16),
             pltpu.VMEM((2, BLOCK, ALLCOLS), BF16),
@@ -649,20 +762,21 @@
             pltpu.VMEM((RING, 8, 512), F32),
             pltpu.VMEM((RING, 8, 512), F32),
             pltpu.VMEM((RING, 8, 512), F32),
-            dma((320,)),
-            dma((2, RING)),
-            dma((2, RING, RING, 2)),
+            dma((400,)),
+            dma((2, RING, 2)),
+            dma((2, RING, 2, RING, 2)),
             dma((2, RING)),
             dma((2, RING, RING, 2)),
             dma((2, RING, 2)),
             dma((2, 2)),
             dma((2, 2, 2)),
+            dma((2, 2, RING, 2)),
             dma((2, RING, 2)),
+            dma((2, 2, RING, 2)),
+            dma((2, 2, RING, 2, 2)),
+            dma((2, 2)),
             dma((2, RING, 2)),
-            dma((2, 2, RING)),
-            dma((2, 2, RING, 2)),
-            dma((2, RING)),
-            dma((1,)),
+            dma((2,)),
             dma((2, 2)),
             dma((2, 2, 2)),
             dma((RING,)),
@@ -679,7 +793,13 @@
         x_saved[0, 0], grad_top[0, 0], query[0, 0], key[0, 0], value[0, 0], segment[0, 0], gain,
         w_query[0], key_weight[0], value_weight[0], w_out[0],
     )
-    bottom, gq, gk, gv, go, gg = outs
+    bottom, gq, gk, gv, go, gg = pl.pallas_call(
+        hand_out,
+        out_shape=tuple(jax.ShapeDtypeStruct(out.shape, out.dtype) for out in outs),
+        in_specs=[vmem] * 6,
+        out_specs=(vmem,) * 6,
+        name="hand_out",
+    )(*outs)
     return (bottom[None, None], gq[None], gk[None], gv[None], go[None], gg)
 
 

time: 203 us -> 192 us (0.946)
  local copies, waits for them, and re-layouts: 5.94 us -> 0 us
  Pallas kernels: 196 us -> 191 us
    pallas_call x1, Pallas kernels: 196 us -> 189 us  [local(): pl.pallas_call(kernel, out_shape=(jax.ShapeDtypeStruct((SUB, WIDTH), BF16...]
    unnamed x16 -> x0, local copies, waits for them, and re-layouts: 5.94 us -> none
    pallas_call x0 -> x1, Pallas kernels: none -> 2.7 us  [local(): pl.pallas_call(hand_out, out_shape=tuple((jax.ShapeDtypeStruct(out.shape,...]
where the time goes in v3:
time: 192 us
  Pallas kernels  191 us (99%)
    pallas_call x1, Pallas kernels, local(): pl.pallas_call(kernel, out_shape=(jax.ShapeDtypeStruct((SUB, WIDTH), BF16...  189 us

profile of v3, /device:TPU:0, one launch (start us, length us, event | category | flops | bytes accessed | tf_op | source)
XLA Modules:
  0.0 192.1 jit_solution(15880657284145557073)
XLA Ops:
  0.6 188.7 %relay_backward.1 = (bf16[64,4096]{1,0:T(8,128)(2,1)}, bf16[256,1024]{1,0:T(8,128)(2,1)}, bf16[256,256]{1,0:T(8,128)(2,1)}, bf16[256,256]{1,0:T(8,128)(2,1)}, bf...) custom-call(bf16[2,64,4096]{2,1,0:T(8,128)(2,1)} %bitcast.15, bf16[64,4096]{1,0:T(8,128)(2,1)} %bitcast.17, ...), custom_call_target="tpu_custom_call" | custom-call | flops 23000000512 | bytes 8000000 | tf_op jit(solution)/shard_map/relay_backward/pallas_call | solution.py:719
  189.4 2.7 %hand_out.1 = (bf16[64,4096]{1,0:T(8,128)(2,1)}, bf16[256,1024]{1,0:T(8,128)(2,1)}, bf16[256,256]{1,0:T(8,128)(2,1)}, bf16[256,256]{1,0:T(8,128)(2,1)}, bf16[256,1024]{1,0:T(8,128)(2,1)}, /*index=5*/f32[1,4096]{1,0:T(1,128)}) custom-call(bf16[64,4096]{1,0:T(8,128)(2,1)} %get-tuple-element.18.refs_0_, bf16[256,1024]{1,0:T(8,128)(2,1)} %get-tuple-element.19.refs_1_, ...), custom_call_target="tpu_custom_call" | custom-call | tf_op jit(solution)/shard_map/hand_out/pallas_call | solution.py:796

commit v4 on v3

--- a/solution.py
+++ b/solution.py
@@ -591,11 +591,11 @@
             qkv_gather.far()
         parts = {(0, 0): grad_normed_rows(m, 0, 0), (0, 1): grad_normed_rows(m, 0, 1)}
         first.forward()
-        for step in (0, 1, 3, 2):
-            nm_gathers[m][step].forward()
         first.near()
         parts[1, 0] = grad_normed_rows(m, 1, 0)
         parts[3, 0] = grad_normed_rows(m, 3, 0)
+        for step in (0, 1, 3, 2):
+            nm_gathers[m][step].forward()
         onward(parts[0, 0])
         onward(parts[0, 1])
         second.forward()
@@ -663,47 +663,47 @@
     qkv_scatter.far()
     qkv_rows(1, 1)
     qkv_scatter.direct(0)
+    for step in (0, 1, 3, 2):
+        grad_normed_sum(1, step, 1, parts[step, 1])
     qkv_rows(1, 3)
     qkv_scatter.direct(1)
     for h in range(2):
         arrived(up_own.at[1, :, own_part(h), :], pipe_sem.at[h])
     grad_normed_back(1, 0)
     grad_input(1, 0)
-    for step in (0, 1, 3, 2):
-        grad_normed_sum(1, step, 1, parts[step, 1])
-    onward(qkv_scatter)
-    out_rows(0)
-    qkv_rows(1, 0)
     grad_normed_back(1, 1)
     grad_input(1, 1)
 
     gain_x[t] = gain_mine[...]
     for o in ORDER:
         send(gain_x.at[t], gain_x.at[t], gx_sem.at[t], dev_x(o))
-    out_scatter.wait()
-    for n in range(4):
-        go_ref[:, cols_of(n)] = summed(pl.ds(DCOLS + n * BLOCK, BLOCK))
+    onward(qkv_scatter)
+    qkv_rows(1, 0)
     for o in ORDER:
         arrived(gain_x.at[plus(t, o)], gx_sem.at[plus(t, o)])
     gain_a[a] = gain_x[0] + gain_x[1] + gain_x[2] + gain_x[3]
     for o in ORDER:
         send(gain_a.at[a], gain_a.at[a], ga_sem.at[a], dev_a(o))
+    out_rows(0)
+    out_scatter.wait()
+    for n in range(4):
+        go_ref[:, cols_of(n)] = summed(pl.ds(DCOLS + n * BLOCK, BLOCK))
     for o in ORDER:
         arrived(gain_a.at[plus(a, o)], ga_sem.at[plus(a, o)])
     gain_b[b] = gain_a[0] + gain_a[1] + gain_a[2] + gain_a[3]
     for o in ORDER:
         send(gain_b.at[b], gain_b.at[b], gb_sem.at[b], dev_b(o))
+    qkv_scatter.wait()
+    for n in range(4):
+        gq_ref[:, cols_of(n)] = summed(cols_of(n))
+    gk_ref[...] = summed(pl.ds(QCOLS, KVCOLS))
+    gv_ref[...] = summed(pl.ds(QCOLS + KVCOLS, KVCOLS))
     for o in ORDER:
         arrived(gain_b.at[plus(b, o)], gb_sem.at[plus(b, o)])
     gain_mine[...] = gain_b[0] + gain_b[1] + gain_b[2] + gain_b[3]
     for i, j in blocks:
         gg_ref[:, at(dp_of(i, j), BLOCK)] = gain_mine[pl.ds(i * 2 + j // 2, 1), cols_of(j % 2)]
 
-    qkv_scatter.wait()
-    for n in range(4):
-        gq_ref[:, cols_of(n)] = summed(cols_of(n))
-    gk_ref[...] = summed(pl.ds(QCOLS, KVCOLS))
-    gv_ref[...] = summed(pl.ds(QCOLS + KVCOLS, KVCOLS))
     finish(list(unfinished.values()))
 
 

time: 192 us -> 196 us (1.021)
  Pallas kernels: 191 us -> 195 us
    pallas_call x1, Pallas kernels: 189 us -> 192 us  [local(): pl.pallas_call(kernel, out_shape=(jax.ShapeDtypeStruct((SUB, WIDTH), BF16...]
where the time goes in v4:
time: 196 us
  Pallas kernels  195 us (99%)
    pallas_call x1, Pallas kernels, local(): pl.pallas_call(kernel, out_shape=(jax.ShapeDtypeStruct((SUB, WIDTH), BF16...  192 us

profile of v4, /device:TPU:0, one launch (start us, length us, event | category | flops | bytes accessed | tf_op | source)
XLA Modules:
  0.0 195.7 jit_solution(17175262718873201212)
XLA Ops:
  0.6 192.4 %relay_backward.1 = (bf16[64,4096]{1,0:T(8,128)(2,1)}, bf16[256,1024]{1,0:T(8,128)(2,1)}, bf16[256,256]{1,0:T(8,128)(2,1)}, bf16[256,256]{1,0:T(8,128)(2,1)}, bf...) custom-call(bf16[2,64,4096]{2,1,0:T(8,128)(2,1)} %bitcast.15, bf16[64,4096]{1,0:T(8,128)(2,1)} %bitcast.17, ...), custom_call_target="tpu_custom_call" | custom-call | flops 23000000512 | bytes 8000000 | tf_op jit(solution)/shard_map/relay_backward/pallas_call | solution.py:719
  193.0 2.7 %hand_out.1 = (bf16[64,4096]{1,0:T(8,128)(2,1)}, bf16[256,1024]{1,0:T(8,128)(2,1)}, bf16[256,256]{1,0:T(8,128)(2,1)}, bf16[256,256]{1,0:T(8,128)(2,1)}, bf16[256,1024]{1,0:T(8,128)(2,1)}, /*index=5*/f32[1,4096]{1,0:T(1,128)}) custom-call(bf16[64,4096]{1,0:T(8,128)(2,1)} %get-tuple-element.18.refs_0_, bf16[256,1024]{1,0:T(8,128)(2,1)} %get-tuple-element.19.refs_1_, ...), custom_call_target="tpu_custom_call" | custom-call | tf_op jit(solution)/shard_map/hand_out/pallas_call | solution.py:796

commit v5 on v4

--- a/solution.py
+++ b/solution.py
@@ -591,11 +591,11 @@
             qkv_gather.far()
         parts = {(0, 0): grad_normed_rows(m, 0, 0), (0, 1): grad_normed_rows(m, 0, 1)}
         first.forward()
+        for step in (0, 1, 3, 2):
+            nm_gathers[m][step].forward()
         first.near()
         parts[1, 0] = grad_normed_rows(m, 1, 0)
         parts[3, 0] = grad_normed_rows(m, 3, 0)
-        for step in (0, 1, 3, 2):
-            nm_gathers[m][step].forward()
         onward(parts[0, 0])
         onward(parts[0, 1])
         second.forward()

time: 196 us -> 190 us (0.969)
  Pallas kernels: 195 us -> 189 us
    pallas_call x1, Pallas kernels: 192 us -> 186 us  [local(): pl.pallas_call(kernel, out_shape=(jax.ShapeDtypeStruct((SUB, WIDTH), BF16...]
where the time goes in v5:
time: 190 us
  Pallas kernels  189 us (99%)
    pallas_call x1, Pallas kernels, local(): pl.pallas_call(kernel, out_shape=(jax.ShapeDtypeStruct((SUB, WIDTH), BF16...  186 us

profile of v5, /device:TPU:0, one launch (start us, length us, event | category | flops | bytes accessed | tf_op | source)
XLA Modules:
  0.0 189.7 jit_solution(17953710241187174297)
XLA Ops:
  0.6 186.4 %relay_backward.1 = (bf16[64,4096]{1,0:T(8,128)(2,1)}, bf16[256,1024]{1,0:T(8,128)(2,1)}, bf16[256,256]{1,0:T(8,128)(2,1)}, bf16[256,256]{1,0:T(8,128)(2,1)}, bf...) custom-call(bf16[2,64,4096]{2,1,0:T(8,128)(2,1)} %bitcast.15, bf16[64,4096]{1,0:T(8,128)(2,1)} %bitcast.17, ...), custom_call_target="tpu_custom_call" | custom-call | flops 23000000512 | bytes 8000000 | tf_op jit(solution)/shard_map/relay_backward/pallas_call | solution.py:719
  187.0 2.7 %hand_out.1 = (bf16[64,4096]{1,0:T(8,128)(2,1)}, bf16[256,1024]{1,0:T(8,128)(2,1)}, bf16[256,256]{1,0:T(8,128)(2,1)}, bf16[256,256]{1,0:T(8,128)(2,1)}, bf16[256,1024]{1,0:T(8,128)(2,1)}, /*index=5*/f32[1,4096]{1,0:T(1,128)}) custom-call(bf16[64,4096]{1,0:T(8,128)(2,1)} %get-tuple-element.18.refs_0_, bf16[256,1024]{1,0:T(8,128)(2,1)} %get-tuple-element.19.refs_1_, ...), custom_call_target="tpu_custom_call" | custom-call | tf_op jit(solution)/shard_map/hand_out/pallas_call | solution.py:796
